TPU v7x, 512 devices: a whole 4x8x8 slice. The times are simulated.
512 devices in a mesh: tm: 16 (over y, core), nin: 8 (over z), nout: 4 (over x).
Axes of the slice: x: 4, y: 8, z: 8, core: 2. Of those that a mesh axis runs over, the one named last changes fastest.
Arguments:
- spikes: int32 [4096, 2048], P('tm', 'nin'), may hold values 0 or 1
- exposure: int32 [4096], P('tm'), may hold values from 1 to 8
- weights: bfloat16 [16384, 2048], P('nin', 'nout'), may hold values from -0.375 to 0.375
- direction: float32 [16384, 2048], P(('nin', 'tm'), 'nout'), may hold values from -6 to 6
- residual: float32 [16384, 2048], P(('nin', 'tm'), 'nout'), may hold values from -0.75 to 0.75
- iterate: float32 [16384, 2048], P(('nin', 'tm'), 'nout'), may hold values from -1.8 to 1.8
Outputs:
- new_iterate: float32 [16384, 2048], P(('nin', 'tm'), 'nout')
- new_residual: float32 [16384, 2048], P(('nin', 'tm'), 'nout')
- new_direction: float32 [16384, 2048], P(('nin', 'tm'), 'nout')
All inputs are finite; a program needn't handle non-finite values. No bound on the sum of `spikes` on one device may be relied on, other than what follows from the above.
Results may differ from a plain program's by a relative error of at most 0.015.
Values may be sent and summed in bfloat16 or wider, within the bound.
A program may use at most 64 MiB of HBM per device.

v0:
```python
import math

import jax
import jax.numpy as jnp
from jax import lax
from jax.sharding import PartitionSpec as P

BASES = 8
HISTORY = 128


RIDGE_WEIGHT = 0.05
NORM_EPS = 1e-06


def shifted(value, axis, steps):
    count = lax.axis_size(axis)
    initial, last = (max(0, -steps), min(count, count - steps))
    return lax.ppermute(value, axis, [(source, source + steps) for source in range(initial, last)])


def basis_table(history, bases_count):
    lag_values = jnp.arange(1, history + 1, dtype=jnp.float32)
    warped = jnp.log(lag_values + 1.0)
    log_low = math.log(2.0)
    log_high = math.log(history + 1.0)
    spacing = (log_high - log_low) / (bases_count - 1)
    centers = log_low + spacing * jnp.arange(bases_count, dtype=jnp.float32)
    phases = (warped[:, None] - centers[None, :]) * (math.pi / (2.0 * spacing))
    phases = jnp.clip(phases, -math.pi, math.pi)
    bump_values = 0.5 * (1.0 + jnp.cos(phases))
    bump_values = bump_values / jnp.sum(bump_values, axis=0, keepdims=True)
    return bump_values.astype(jnp.bfloat16)


def lag_kernel(basis_rows, span, offset):
    out_index = jnp.arange(span, dtype=jnp.int32)[:, None]
    in_index = jnp.arange(span, dtype=jnp.int32)[None, :]
    lag_index = out_index + offset - in_index
    is_valid = (lag_index >= 1) & (lag_index <= HISTORY)
    take_index = jnp.clip(lag_index - 1, 0, HISTORY - 1)
    return jnp.where(
        is_valid[None], jnp.take(basis_rows.T, take_index, axis=1), jnp.zeros((), jnp.bfloat16)
    )


def per_device(spikes, exposure, weights, direction, residual, iterate):
    block_rows = spikes.shape[0]
    neuron_cols = spikes.shape[1]
    basis_rows = basis_table(HISTORY, BASES)
    spike_low = spikes.astype(jnp.bfloat16)
    block_count = block_rows // HISTORY
    stacked = spike_low.reshape(block_count, HISTORY, neuron_cols)
    kernel_same = lag_kernel(basis_rows, HISTORY, 0)
    kernel_before = lag_kernel(basis_rows, HISTORY, HISTORY)
    current = jnp.einsum("bim,cmn->cinb", kernel_same, stacked, preferred_element_type=jnp.float32)
    tail_part = jnp.einsum(
        "bim,mn->inb", kernel_before, stacked[-1], preferred_element_type=jnp.float32
    )
    inner_part = jnp.einsum(
        "bim,cmn->cinb", kernel_before, stacked[:-1], preferred_element_type=jnp.float32
    )
    tail_terms = shifted(tail_part.astype(jnp.bfloat16), "tm", 1).astype(tail_part.dtype)
    own_terms = current + jnp.concatenate([tail_terms[None], inner_part], axis=0)
    features = own_terms.reshape(block_rows, neuron_cols * BASES).astype(jnp.bfloat16)
    direction_low = direction.astype(jnp.bfloat16)
    columns = features
    along_part = jnp.dot(
        columns,
        lax.all_gather(direction_low, "tm", axis=0, tiled=True),
        preferred_element_type=jnp.float32,
    )
    predictor_part = jnp.dot(features, weights, preferred_element_type=jnp.float32)
    tick_scale = exposure.astype(jnp.float32) / 8.0
    predictor_full, along_full = (
        lax.psum(predictor_part.astype(jnp.bfloat16), "nin").astype(jnp.float32),
        lax.psum(along_part.astype(jnp.bfloat16), "nin").astype(jnp.float32),
    )
    weighted = (tick_scale[:, None] * jnp.exp(predictor_full) * along_full).astype(jnp.bfloat16)
    columns = features
    gram = lax.psum_scatter(
        lax.dot_general(
            columns, weighted, (((0,), (0,)), ((), ())), preferred_element_type=jnp.float32
        ).astype(jnp.bfloat16),
        "tm",
        scatter_dimension=0,
        tiled=True,
    ).astype(jnp.float32)
    bin_total = block_rows * lax.axis_size("tm")
    curvature_prod = gram / bin_total + RIDGE_WEIGHT * direction
    old_norm, curvature = lax.psum(
        (jnp.sum(residual * residual, axis=0), jnp.sum(direction * curvature_prod, axis=0)),
        ("tm", "nin"),
    )
    step_size = old_norm / curvature
    new_iterate = iterate + step_size[None, :] * direction
    new_residual = residual - step_size[None, :] * curvature_prod
    new_norm = lax.psum(jnp.sum(new_residual * new_residual, axis=0), ("tm", "nin"))
    new_direction = new_residual + (new_norm / (old_norm + NORM_EPS))[None, :] * direction
    return (new_iterate, new_residual, new_direction)


def solution(mesh):
    in_specs = (
        P("tm", "nin"),
        P("tm"),
        P("nin", "nout"),
        P(("nin", "tm"), "nout"),
        P(("nin", "tm"), "nout"),
        P(("nin", "tm"), "nout"),
    )
    out_specs = (P(("nin", "tm"), "nout"), P(("nin", "tm"), "nout"), P(("nin", "tm"), "nout"))
    return jax.shard_map(
        per_device, mesh=mesh, in_specs=in_specs, out_specs=out_specs, check_vma=False
    )
```

profile of v0, /device:TPU:1, one launch (start us, length us, event | category | flops | bytes accessed | tf_op | source)
XLA Modules:
  0.0 792.6 jit_solution(18235166921538115580)
XLA Ops:
  7.2 0.0 copy-start
  7.2 0.0 all-gather.2.cloned.1.call-start
  7.2 1.8 convert_element_type.56
  9.0 0.0 all-gather.2.cloned.1.call-update
  9.0 0.0 all-reduce.4.cloned.1.call-start
  9.1 0.2 multiply_reduce_fusion.3
  9.3 0.1 divide_convert_fusion
  9.4 0.1 copy.17
  9.6 0.1 bitcast_clamp_fusion
  9.7 57.8 %gather_fusion.1 = bf16[16384,8]{1,0:T(8,128)(2,1)} fusion(bf16[8,128]{0,1:T(8,128)(2,1)S(1)} %copy.17, s32[16384]{0:T(1024)S(1)} %bitcast_clamp_fusion), kind=kCustom, calls=%fused_computation.1.clone | custom fusion | bytes 589824 | tf_op jit(solution)/shard_map/jit(_take)/gather | solution.py:43
  67.5 0.0 copy-start.5
  67.5 3.6 copy.20
  71.2 0.0 copy-done.5
  71.2 0.1 fusion.30
  71.3 1.1 fusion.1
  72.4 4.6 collective-permute-start
  77.0 57.8 %gather_fusion = bf16[16384,8]{1,0:T(8,128)(2,1)} fusion(bf16[8,128]{0,1:T(8,128)(2,1)S(1)} %copy.17, s32[16384]{0:T(1024)S(1)} %bitcast_clamp_fusion.1), kind=kCustom, calls=%fused_computation.clone | custom fusion | bytes 589824 | tf_op jit(solution)/shard_map/jit(_take)/gather | solution.py:43
  134.8 3.6 copy.18
  138.4 0.1 fusion.27
  138.5 0.3 convolution_bitcast_fusion
  138.8 0.0 collective-permute-done
  138.8 0.1 bitcast_convert_fusion
  138.9 0.4 fusion
  139.3 2.1 copy.21
  141.4 0.0 copy-done
  141.4 0.0 copy-start.2
  141.4 2.8 convolution_convert_fusion.3
  144.2 0.0 copy-start.7
  144.2 0.0 all-gather.2.cloned.1.call-done
  144.2 0.0 copy-done.2
  144.2 3.1 convolution_convert_fusion.2
  147.3 0.0 all-reduce.4.cloned.1.call-update
  147.3 0.0 reduce-scatter.2.cloned.1.call-start
  147.3 0.0 copy-done.7
  147.3 78.7 %all-reduce.4.cloned.1.call-done = (bf16[256,512]{1,0:T(8,128)(2,1)}, bf16[256,512]{1,0:T(8,128)(2,1)}) async-done(((bf16[256,512]{1,0:T(8,128)(2,1)}, bf16[256,512]{1,0:T(8,128)(2,1)}), (bf16[256,512]{1,0:T(8,128)(2,1)}, bf16[256,512]{1,0:T(8,128)(2,1)})) %all-reduce.4.cloned.1.call-update) | async-done | bytes 524304 | tf_op jit(solution)/shard_map/psum | solution.py:77
  226.1 0.0 copy-start.4
  226.1 3.2 convolution_convert_fusion
  229.3 0.0 copy-start.1
  229.3 0.0 copy-start.6
  229.3 0.0 reduce-scatter.2.cloned.1.call-update
  229.3 0.0 copy-done.4
  229.4 62.3 %reduce-scatter.2.cloned.1.call-done = bf16[128,512]{1,0:T(8,128)(2,1)} async-done(((bf16[2048,512]{1,0:T(8,128)(2,1)}), bf16[128,512]{1,0:T(8,128)(2,1)}) %reduce-scatter.2.cloned.1.call-update) | async-done | bytes 131088 | tf_op jit(solution)/shard_map/reduce_scatter | solution.py:81
  291.7 0.0 copy-done.1
  291.7 1.0 multiply_reduce_fusion.1
  292.6 244.2 %all-reduce = (f32[512]{0:T(512)S(1)}, f32[512]{0:T(512)S(1)}) all-reduce(f32[512]{0:T(512)S(1)} %multiply_reduce_fusion.2, f32[512]{0:T(512)S(1)} %multiply_reduce_fusion.1), channel_id=1, replica_groups=mesh['tm'=16,'nin'=8,'nout'=4] {'tm','nin'}, use_global_device_ids=true, to_apply=%region_1.2 | all-reduce | flops 1024 | bytes 8192 | tf_op jit(solution)/shard_map/psum | solution.py:91
  536.9 0.0 copy-done.6
  536.9 1.7 multiply_reduce_fusion
  538.6 0.0 copy-start.3
  538.6 246.8 %psum.39 = f32[512]{0:T(512)S(1)} all-reduce(f32[512]{0:T(512)S(1)} %get-tuple-element.8), channel_id=1, replica_groups=mesh['tm'=16,'nin'=8,'nout'=4] {'tm','nin'}, use_global_device_ids=true, to_apply=%region_9.11 | all-reduce | flops 512 | bytes 4096 | tf_op jit(solution)/shard_map/psum | solution.py:98
  785.4 0.8 multiply_add_fusion
  786.1 0.0 copy-done.3
  (9 shorter events, 0.1 us)
Async XLA Ops:
  7.2 134.3 %copy-start = (bf16[2048,512]{1,0:T(8,128)(2,1)S(1)}, bf16[2048,512]{1,0:T(8,128)(2,1)}, u32[]{:S(2)}) copy-start(bf16[2048,512]{1,0:T(8,128)(2,1)} %param.10) | copy-start | bytes 6291460
  7.2 137.0 %all-gather.2.cloned.1.call-start = ((), (), s32[]{:S(2)}) async-start(), calls=%async_computation.1 | async-start | bytes 2228224 | tf_op jit(solution)/shard_map/all_gather | solution.py:70
  9.0 217.0 %all-reduce.4.cloned.1.call-start = ((), (), s32[]{:S(2)}) async-start(), calls=%async_computation.3 | async-start | bytes 1048576 | tf_op jit(solution)/shard_map/psum | solution.py:77
  67.5 3.6 copy-start.5
  72.4 66.4 %collective-permute-start = (bf16[128,256,8]{1,0,2:T(8,128)(2,1)}, bf16[128,256,8]{1,0,2:T(8,128)(2,1)S(1)}, u32[]{:S(2)}, u32[]{:S(2)}) collective-permute-start(bf16[128,256,8]{1,0,2:T(8,128)(2,1)} %fusion.1), channel_id=1, source_target_pairs={{0,32},{32,64},{64,96},{96,128},{128,160},{160,192},{192,224},{224... | collective-permute-start | bytes 1572872 | tf_op jit(solution)/shard_map/ppermute | solution.py:19
  141.4 2.8 copy-start.2
  144.2 3.1 copy-start.7
  147.3 144.4 %reduce-scatter.2.cloned.1.call-start = ((), (), s32[]{:S(2)}) async-start(), calls=%async_computation.2 | async-start | bytes 2228224 | tf_op jit(solution)/shard_map/reduce_scatter | solution.py:81
  226.1 3.3 copy-start.4
  229.3 62.4 %copy-start.1 = (f32[128,512]{1,0:T(8,128)S(1)}, f32[128,512]{1,0:T(8,128)}, u32[]{:S(2)}) copy-start(f32[128,512]{1,0:T(8,128)} %param.11) | copy-start | bytes 786436
  229.3 307.6 %copy-start.6 = (f32[128,512]{1,0:T(8,128)S(1)}, f32[128,512]{1,0:T(8,128)}, u32[]{:S(2)}) copy-start(f32[128,512]{1,0:T(8,128)} %param.13) | copy-start | bytes 786436
  538.6 247.6 %copy-start.3 = (f32[128,512]{1,0:T(8,128)}, f32[128,512]{1,0:T(8,128)S(1)}, u32[]{:S(2)}) copy-start(f32[128,512]{1,0:T(8,128)S(1)} %get-tuple-element.9) | copy-start | bytes 786436
Sparse Core Ops, SparseCore 0:
  10.7 47.7 all-gather.1
  147.4 78.6 all-reduce.3
  229.4 62.1 reduce-scatter.1
where the time goes:
time: 800 us; the launch traced here: 793 us
  blocking collectives  491 us (61%)
  waiting for transfers between devices  141 us (18%)
  local copies, waits for them, and re-layouts  125 us (16%)
  between operations  13.9 us (2%)
  matrix products  10.8 us (1%)
    psum x1, blocking collectives, per_device(): lax.psum(jnp.sum(new_residual * new_residual, axis=0), ('tm', 'nin'))  247 us
    psum x1, blocking collectives, per_device(): lax.psum((jnp.sum(residual * residual, axis=0), jnp.sum(direction * curva...  244 us
    gather x4, local copies, waits for them, and re-layouts, lag_kernel(): jnp.take(basis_rows.T, take_index, axis=1)  123 us
    psum x1, waiting for transfers between devices, per_device(): lax.psum(along_part.astype(jnp.bfloat16), 'nin').astype(jnp.float32)  78.7 us
    reduce_scatter x1, waiting for transfers between devices, per_device(): lax.psum_scatter(lax.dot_general(columns, weighted, (((0,), (0,)), ((), (...  62.3 us
  transfers between devices with their start and end apart: 4, of which 2 were waited for; matrix products, arithmetic and copies ran while one was open for 16% of the time, Pallas kernels for 0%

commit v1 on v0

v1 whole, which is shorter than its diff:
```python
import functools
import math

import jax
import jax.numpy as jnp
import numpy as np
from jax import lax
from jax.experimental import pallas as pl
from jax.experimental.pallas import tpu as pltpu
from jax.sharding import PartitionSpec as P

BASES = 8
HISTORY = 128
RIDGE_WEIGHT = 0.05
NORM_EPS = 1e-06
MESH = pl.DeviceIdType.MESH
F32 = jnp.float32
BF16 = jnp.bfloat16

TM = 16
NIN = 8
GROUP = 4
BINS = 1024
OWN = 256
NEUR = 256
COLS = 128
FEAT = NEUR * BASES
SLOT = NEUR // TM


def basis_table():
    lag_values = np.arange(1, HISTORY + 1, dtype=np.float32)
    warped = np.log(lag_values + np.float32(1.0))
    log_low = math.log(2.0)
    log_high = math.log(HISTORY + 1.0)
    spacing = (log_high - log_low) / (BASES - 1)
    centers = np.float32(log_low) + np.float32(spacing) * np.arange(BASES, dtype=np.float32)
    phases = (warped[:, None] - centers[None, :]) * np.float32(math.pi / (2.0 * spacing))
    phases = np.clip(phases, np.float32(-math.pi), np.float32(math.pi))
    bumps = np.float32(0.5) * (np.float32(1.0) + np.cos(phases))
    bumps = bumps / np.sum(bumps, axis=0, keepdims=True)
    return bumps.astype(np.float32)


def lag_table():
    basis = basis_table()
    lag = np.arange(HISTORY)[:, None] + HISTORY - np.arange(2 * HISTORY)[None, :]
    valid = (lag >= 1) & (lag <= HISTORY)
    table = np.where(valid[None], basis.T[:, np.clip(lag - 1, 0, HISTORY - 1)], np.float32(0.0))
    return table.reshape(BASES * HISTORY, 2 * HISTORY)


def kernel(
    exposure_ref, spikes_hbm, weights_hbm, direction_hbm, residual_hbm, iterate_hbm, lag_hbm, lag_t_hbm,
    iterate_out, residual_out, direction_out,
    spikes_in, lag, lag_t, d32, r32, it32, w16, w32, wp, spk, spk_t, x, xt,
    d_send, d_all, p_own, p_send, p_recv, a_own, a_send, a_recv, wt_all, g_send, g_recv, g_nat,
    ticks, ticks_t, nd_send, nd_recv, cv_send, cv_recv, c2_send, c2_recv, nn_send, nn_recv, nz_send, nz_recv,
    load_sem, spk_sem, halo_sem, tick_sem, d_sem, p_sem, a_sem, wt_sem, g_sem, nd_sem, cv_sem, c2_sem, nn_sem, nz_sem,
):
    me = lax.axis_index("tm")
    z = lax.axis_index("nin")
    xo = lax.axis_index("nout")
    team = me // GROUP
    part = lax.rem(me, GROUP)

    def tm_peer(step):
        return lax.rem(me + step, TM)

    def z_peer(step):
        return lax.rem(z + step, NIN)

    def team_peer(step):
        return team * GROUP + lax.rem(part + step, GROUP)

    def remote(src, dst, sems, slot, tm_index, z_index):
        return pltpu.make_async_remote_copy(
            src_ref=src, dst_ref=dst, send_sem=sems.at[0, slot], recv_sem=sems.at[1, slot],
            device_id=(tm_index, z_index, xo), device_id_type=MESH,
        )

    def each(first, last, body):
        def run(step, carry):
            body(step)
            return carry

        lax.fori_loop(first, last, run, 0)

    loads = [
        pltpu.make_async_copy(spikes_hbm, spikes_in, load_sem.at[0]),
        pltpu.make_async_copy(lag_hbm, lag, load_sem.at[1]),
        pltpu.make_async_copy(lag_t_hbm, lag_t, load_sem.at[2]),
        pltpu.make_async_copy(
            weights_hbm.at[:, pl.ds(pl.multiple_of(part * COLS, COLS), COLS)], w16, load_sem.at[3]
        ),
    ]
    blocks = [
        [
            pltpu.make_async_copy(source.at[:, k * COLS : (k + 1) * COLS], target.at[k], load_sem.at[4 + 4 * n + k])
            for k in range(GROUP)
        ]
        for n, (source, target) in enumerate(((direction_hbm, d32), (residual_hbm, r32), (iterate_hbm, it32)))
    ]
    for copy in blocks[0] + loads[:1]:
        copy.start()
    for copy in loads[1:] + blocks[1] + blocks[2]:
        copy.start()

    barrier = pltpu.get_barrier_semaphore()

    def greet_tm(step):
        pl.semaphore_signal(barrier, inc=1, device_id=(tm_peer(step), z, xo), device_id_type=MESH)

    def greet_z(step):
        pl.semaphore_signal(barrier, inc=1, device_id=(me, z_peer(step), xo), device_id_type=MESH)

    each(1, TM, greet_tm)
    each(1, NIN, greet_z)

    for copy in blocks[0]:
        copy.wait()
    for k in range(GROUP):
        for b in range(BASES):
            d_send[k, b] = d32[k, pl.ds(b, SLOT, stride=BASES), :].astype(BF16)
    loads[0].wait()
    own_rows = pl.ds(pl.multiple_of(HISTORY + part * OWN, HISTORY), OWN)
    spk[own_rows, :] = spikes_in[...].astype(F32).astype(BF16)
    ticks[part, 0:2, :] = exposure_ref[...].astype(F32) / 8.0
    ticks[part, 2:8, :] = jnp.zeros((6, COLS), F32)
    pl.semaphore_wait(barrier, TM - 1 + NIN - 1)

    def spikes_copy(step):
        return remote(spk.at[own_rows], spk.at[own_rows], spk_sem, step, team_peer(step), z)

    def spikes_arrival(step):
        rows = pl.ds(pl.multiple_of(HISTORY + lax.rem(part + GROUP - step, GROUP) * OWN, HISTORY), OWN)
        return remote(spk.at[rows], spk.at[rows], spk_sem, step, team_peer(step), z)

    def halo_copy(k):
        return remote(
            spk.at[BINS : BINS + HISTORY], spk.at[0:HISTORY], halo_sem, k, lax.rem((team + 1) * GROUP + k, TM), z
        )

    def tick_copy(step):
        return remote(ticks.at[part], ticks.at[part], tick_sem, step, team_peer(step), z)

    def tick_arrival(step):
        slot = lax.rem(part + GROUP - step, GROUP)
        return remote(ticks.at[slot], ticks.at[slot], tick_sem, step, team_peer(step), z)

    d_rows = pl.ds(pl.multiple_of(me * SLOT, SLOT), SLOT)

    def direction_copy(step):
        peer = tm_peer(step)
        return remote(d_send.at[lax.rem(peer, GROUP)], d_all.at[:, d_rows, :], d_sem, step, peer, z)

    def direction_arrival(step):
        rows = pl.ds(pl.multiple_of(tm_peer(TM - step) * SLOT, SLOT), SLOT)
        return remote(d_send.at[0], d_all.at[:, rows, :], d_sem, step, tm_peer(step), z)

    sends_halo = jnp.logical_and(part == GROUP - 1, team < TM // GROUP - 1)

    each(1, GROUP, lambda step: spikes_copy(step).start())

    @pl.when(sends_halo)
    def _():
        each(0, GROUP, lambda k: halo_copy(k).start())

    each(1, TM, lambda step: direction_copy(step).start())
    each(1, GROUP, lambda step: tick_copy(step).start())
    d_all[:, d_rows, :] = d_send[part]

    for copy in blocks[1]:
        copy.wait()
    for k in range(GROUP):
        nd_send[k : k + 1, :] = jnp.sum(r32[k] * r32[k], axis=0, keepdims=True)
        nd_send[GROUP + k : GROUP + k + 1, :] = jnp.sum(d32[k] * d32[k], axis=0, keepdims=True)

    def nd_copy(step):
        return remote(nd_send, nd_recv.at[step], nd_sem, step, tm_peer(step), z)

    each(1, TM, lambda step: nd_copy(step).start())

    loads[3].wait()
    w32[...] = w16[...].astype(F32)
    for b in range(BASES):
        wp[b * NEUR : (b + 1) * NEUR, :] = w32[pl.ds(b, NEUR, stride=BASES), :].astype(BF16)
    loads[1].wait()
    loads[2].wait()

    @pl.when(team == 0)
    def _():
        spk[0:HISTORY, :] = jnp.zeros((HISTORY, NEUR), BF16)

    @pl.when(team > 0)
    def _():
        pltpu.make_async_remote_copy(
            src_ref=spk.at[0:HISTORY], dst_ref=spk.at[0:HISTORY], send_sem=halo_sem.at[0, part],
            recv_sem=halo_sem.at[1, part], device_id=(me, z, xo), device_id_type=MESH,
        ).wait_recv()

    each(1, GROUP, lambda step: spikes_arrival(step).wait_recv())

    for n in range(9):
        spk_t[:, n * HISTORY : (n + 1) * HISTORY] = spk[n * HISTORY : (n + 1) * HISTORY, :].astype(F32).T.astype(BF16)

    def features(block):
        rows = pl.ds(pl.multiple_of(block * HISTORY, HISTORY), HISTORY)
        window = pl.ds(pl.multiple_of(block * HISTORY, HISTORY), 2 * HISTORY)
        made = jnp.dot(lag[...], spk[window, :], preferred_element_type=F32)
        for b in range(BASES):
            x[rows, b * NEUR : (b + 1) * NEUR] = made[b * HISTORY : (b + 1) * HISTORY].astype(BF16)
        made_t = jnp.dot(spk_t[:, window], lag_t[...], preferred_element_type=F32)
        for b in range(BASES):
            piece = made_t[:, b * HISTORY : (b + 1) * HISTORY].astype(BF16)
            xt[:, b, :, rows] = piece.reshape(TM, SLOT, HISTORY)

    each(0, BINS // HISTORY, features)

    def predictor(half):
        rows = pl.ds(pl.multiple_of(half * 512, 512), 512)
        made = jnp.dot(x[rows, :], wp[...], preferred_element_type=F32).reshape(NIN, 64, COLS)
        p_own[half] = made
        p_send[half] = made.astype(BF16)

    each(0, 2, predictor)

    def predictor_copy(step):
        return remote(p_send.at[:, z_peer(step)], p_recv.at[:, step], p_sem, step, me, z_peer(step))

    each(1, NIN, lambda step: predictor_copy(step).start())

    each(1, TM, lambda step: direction_arrival(step).wait_recv())

    def along_copy(half, step):
        return remote(a_send.at[half, z_peer(step)], a_recv.at[half, step], a_sem, half * NIN + step, me, z_peer(step))

    def along(half):
        rows = pl.ds(pl.multiple_of(half * 512, 512), 512)
        made = jnp.dot(x[rows, :], d_all[...].reshape(FEAT, COLS), preferred_element_type=F32).reshape(NIN, 64, COLS)
        a_own[half] = made
        a_send[half] = made.astype(BF16)
        each(1, NIN, lambda step: along_copy(half, step).start())

    each(0, 2, along)

    each(1, GROUP, lambda step: tick_arrival(step).wait_recv())
    table = jnp.concatenate([ticks[k, 0:2, :] for k in range(GROUP)] + [jnp.zeros((COLS - 8, COLS), F32)], axis=0)
    ticks_t[...] = table.T
    tick_rows = ticks_t[pl.ds(pl.multiple_of(lax.rem(z, 2) * 64, 64), 64), :]
    lane = lax.broadcasted_iota(jnp.int32, (64, COLS), 1)

    each(1, TM, lambda step: nd_copy(step).wait_recv())
    cv_send[0:8, :] = nd_send[...] + jnp.sum(nd_recv[1:TM], axis=0)

    each(1, NIN, lambda step: predictor_copy(step).wait_recv())
    curvature_part = jnp.zeros((1, COLS), F32)
    for half in range(2):
        each(1, NIN, lambda step: along_copy(half, step).wait_recv())
        p_sum = p_own[half, z]
        a_sum = a_own[half, z]
        for step in range(1, NIN):
            p_sum += p_recv[half, step].astype(F32)
            a_sum += a_recv[half, step].astype(F32)
        scale = jnp.sum(jnp.where(lane == half * 4 + z // 2, tick_rows, 0.0), axis=1, keepdims=True)
        weighted = ((scale * jnp.exp(p_sum)) * a_sum).astype(BF16)
        wt_all[half, z] = weighted
        each(
            1, NIN,
            lambda step: remote(
                wt_all.at[half, z], wt_all.at[half, z], wt_sem, half * NIN + step, me, z_peer(step)
            ).start(),
        )
        curvature_part += jnp.sum(weighted.astype(F32) * a_sum, axis=0, keepdims=True)
    cv_send[8:16, :] = jnp.concatenate([curvature_part, jnp.zeros((7, COLS), F32)], axis=0)

    def cv_copy(step):
        return remote(cv_send, cv_recv.at[step], cv_sem, step, me, z_peer(step))

    each(1, NIN, lambda step: cv_copy(step).start())

    def weighted_arrival(half, step):
        slot = z_peer(NIN - step)
        return remote(wt_all.at[half, slot], wt_all.at[half, slot], wt_sem, half * NIN + step, me, z_peer(step))

    for half in range(2):
        each(1, NIN, lambda step: weighted_arrival(half, step).wait_recv())

    def gram_copy(step):
        return remote(g_send.at[tm_peer(step)], g_recv.at[me], g_sem, step, tm_peer(step), z)

    def gram_arrival(step):
        return remote(g_send.at[0], g_recv.at[tm_peer(TM - step)], g_sem, step, tm_peer(step), z)

    def gram(slots):
        rows = pl.ds(slots * 4, 4)
        made = jnp.dot(
            xt[rows].reshape(4 * SLOT * BASES, BINS), wt_all[...].reshape(BINS, COLS), preferred_element_type=F32
        )
        g_send[rows] = made.astype(BF16).reshape(4, SLOT * BASES, COLS)

    each(0, 4, gram)
    each(1, TM, lambda step: gram_copy(step).start())
    g_recv[me] = g_send[me]

    each(1, NIN, lambda step: cv_copy(step).wait_recv())
    cv_sum = cv_send[...] + jnp.sum(cv_recv[1:NIN], axis=0)
    old_norm = cv_sum[0:4, :]
    c2_send[...] = cv_sum[8:16, :]
    c2_recv[me] = cv_sum[8:16, :]

    def c2_copy(step):
        return remote(c2_send, c2_recv.at[me], c2_sem, step, tm_peer(step), z)

    def c2_arrival(step):
        return remote(c2_send, c2_recv.at[tm_peer(TM - step)], c2_sem, step, tm_peer(step), z)

    each(1, TM, lambda step: c2_copy(step).start())
    each(1, TM, lambda step: c2_arrival(step).wait_recv())
    for copy in blocks[2]:
        copy.wait()
    step_sizes = []
    for k in range(GROUP):
        total = c2_recv[k, 0:1, :]
        for t in range(1, TM // GROUP):
            total += c2_recv[t * GROUP + k, 0:1, :]
        curvature = total / (BINS * (TM // GROUP)) + RIDGE_WEIGHT * cv_sum[4 + k : 5 + k, :]
        step_size = old_norm[k : k + 1, :] / curvature
        step_sizes.append(step_size)
        iterate_out[:, k * COLS : (k + 1) * COLS] = it32[k] + step_size * d32[k]

    each(1, TM, lambda step: gram_arrival(step).wait_recv())
    nn_send[4:8, :] = jnp.zeros((4, COLS), F32)
    for k in range(GROUP):
        total = g_recv[k].astype(F32)
        for t in range(1, TM // GROUP):
            total += g_recv[t * GROUP + k].astype(F32)
        for b in range(BASES):
            g_nat[k, pl.ds(b, SLOT, stride=BASES), :] = total[b * SLOT : (b + 1) * SLOT]
        product = g_nat[k] / (BINS * (TM // GROUP)) + RIDGE_WEIGHT * d32[k]
        new_residual = r32[k] - step_sizes[k] * product
        residual_out[:, k * COLS : (k + 1) * COLS] = new_residual
        nn_send[k : k + 1, :] = jnp.sum(new_residual * new_residual, axis=0, keepdims=True)

    def nn_copy(step):
        return remote(nn_send, nn_recv.at[step], nn_sem, step, tm_peer(step), z)

    each(1, TM, lambda step: nn_copy(step).start())
    each(1, TM, lambda step: nn_copy(step).wait_recv())
    nz_send[...] = nn_send[...] + jnp.sum(nn_recv[1:TM], axis=0)

    def nz_copy(step):
        return remote(nz_send, nz_recv.at[step], nz_sem, step, me, z_peer(step))

    each(1, NIN, lambda step: nz_copy(step).start())
    each(1, NIN, lambda step: nz_copy(step).wait_recv())
    new_norm = nz_send[...] + jnp.sum(nz_recv[1:NIN], axis=0)
    for k in range(GROUP):
        columns = slice(k * COLS, (k + 1) * COLS)
        ratio = new_norm[k : k + 1, :] / (old_norm[k : k + 1, :] + NORM_EPS)
        direction_out[:, columns] = residual_out[:, columns] + ratio * d32[k]

    each(1, GROUP, lambda step: spikes_copy(step).wait_send())

    @pl.when(sends_halo)
    def _():
        each(0, GROUP, lambda k: halo_copy(k).wait_send())

    each(1, GROUP, lambda step: tick_copy(step).wait_send())
    for copy in (direction_copy, nd_copy, gram_copy, c2_copy, nn_copy):
        each(1, TM, lambda step: copy(step).wait_send())
    for copy in (predictor_copy, cv_copy, nz_copy):
        each(1, NIN, lambda step: copy(step).wait_send())
    for half in range(2):
        each(1, NIN, lambda step: along_copy(half, step).wait_send())
        each(1, NIN, lambda step: weighted_arrival(half, step).wait_send())


def per_device(spikes, exposure, weights, direction, residual, iterate):
    table = lag_table()
    lag = jnp.asarray(table, BF16)
    lag_t = jnp.asarray(np.ascontiguousarray(table.T), BF16)
    rows, columns = direction.shape
    vmem = pl.BlockSpec(memory_space=pltpu.VMEM)
    hbm = pl.BlockSpec(memory_space=pl.ANY)
    pair = lambda n: pltpu.SemaphoreType.DMA((2, n))
    scratch = [
        pltpu.VMEM((OWN, NEUR), jnp.int32),
        pltpu.VMEM((BASES * HISTORY, 2 * HISTORY), BF16),
        pltpu.VMEM((2 * HISTORY, BASES * HISTORY), BF16),
        pltpu.VMEM((GROUP, rows, COLS), F32),
        pltpu.VMEM((GROUP, rows, COLS), F32),
        pltpu.VMEM((GROUP, rows, COLS), F32),
        pltpu.VMEM((FEAT, COLS), BF16),
        pltpu.VMEM((FEAT, COLS), F32),
        pltpu.VMEM((FEAT, COLS), BF16),
        pltpu.VMEM((HISTORY + BINS, NEUR), BF16),
        pltpu.VMEM((NEUR, HISTORY + BINS), BF16),
        pltpu.VMEM((BINS, FEAT), BF16),
        pltpu.VMEM((TM, BASES, SLOT, BINS), BF16),
        pltpu.VMEM((GROUP, BASES, SLOT, COLS), BF16),
        pltpu.VMEM((BASES, NEUR, COLS), BF16),
        pltpu.VMEM((2, NIN, 64, COLS), F32),
        pltpu.VMEM((2, NIN, 64, COLS), BF16),
        pltpu.VMEM((2, NIN, 64, COLS), BF16),
        pltpu.VMEM((2, NIN, 64, COLS), F32),
        pltpu.VMEM((2, NIN, 64, COLS), BF16),
        pltpu.VMEM((2, NIN, 64, COLS), BF16),
        pltpu.VMEM((2, NIN, 64, COLS), BF16),
        pltpu.VMEM((TM, rows, COLS), BF16),
        pltpu.VMEM((TM, rows, COLS), BF16),
        pltpu.VMEM((GROUP, rows, COLS), F32),
        pltpu.VMEM((GROUP, 8, COLS), F32),
        pltpu.VMEM((COLS, COLS), F32),
        pltpu.VMEM((8, COLS), F32),
        pltpu.VMEM((TM, 8, COLS), F32),
        pltpu.VMEM((16, COLS), F32),
        pltpu.VMEM((NIN, 16, COLS), F32),
        pltpu.VMEM((8, COLS), F32),
        pltpu.VMEM((TM, 8, COLS), F32),
        pltpu.VMEM((8, COLS), F32),
        pltpu.VMEM((TM, 8, COLS), F32),
        pltpu.VMEM((8, COLS), F32),
        pltpu.VMEM((NIN, 8, COLS), F32),
        pltpu.SemaphoreType.DMA((16,)),
        pair(GROUP), pair(GROUP), pair(GROUP),
        pair(TM), pair(NIN), pair(2 * NIN), pair(2 * NIN), pair(TM),
        pair(TM), pair(NIN), pair(TM), pair(TM), pair(NIN),
    ]
    return pl.pallas_call(
        kernel,
        out_shape=[jax.ShapeDtypeStruct((rows, columns), F32)] * 3,
        in_specs=[vmem] + [hbm] * 7,
        out_specs=[vmem] * 3,
        scratch_shapes=scratch,
        compiler_params=pltpu.CompilerParams(
            collective_id=0, has_side_effects=True, vmem_limit_bytes=40 * 2**20
        ),
    )(exposure.reshape(2, COLS), spikes, weights, direction, residual, iterate, lag, lag_t)


def solution(mesh):
    in_specs = (
        P("tm", "nin"),
        P("tm"),
        P("nin", "nout"),
        P(("nin", "tm"), "nout"),
        P(("nin", "tm"), "nout"),
        P(("nin", "tm"), "nout"),
    )
    out_specs = (P(("nin", "tm"), "nout"), P(("nin", "tm"), "nout"), P(("nin", "tm"), "nout"))
    return jax.shard_map(
        per_device, mesh=mesh, in_specs=in_specs, out_specs=out_specs, check_vma=False
    )
```

time: 800 us -> 94.3 us (0.12)
  blocking collectives: 491 us -> 0 us
  waiting for transfers between devices: 141 us -> 0 us
  local copies, waits for them, and re-layouts: 125 us -> 10.3 us
  Pallas kernels: 0 us -> 83 us
  between operations: 13.9 us -> 0.66 us
  matrix products: 10.8 us -> 0 us
    psum x2 -> x0, blocking collectives: 491 us -> none  [the longest x1 247 us: per_device(): lax.psum(jnp.sum(new_residual * new_residual, axis=0), ('tm', 'nin'))]
    gather x4 -> x0, local copies, waits for them, and re-layouts: 123 us -> none  [lag_kernel(): jnp.take(basis_rows.T, take_index, axis=1)]
    pallas_call x0 -> x1, Pallas kernels: none -> 83 us  [per_device(): pl.pallas_call(kernel, out_shape=[jax.ShapeDtypeStruct((rows, columns), F...]
    psum x1 -> x0, waiting for transfers between devices: 78.7 us -> none  [per_device(): lax.psum(along_part.astype(jnp.bfloat16), 'nin').astype(jnp.float32)]
    reduce_scatter x1 -> x0, waiting for transfers between devices: 62.3 us -> none  [per_device(): lax.psum_scatter(lax.dot_general(columns, weighted, (((0,), (0,)), ((), (...]
    dot_general x6 -> x0, matrix products: 10.8 us -> none  [the longest x1 3.23 us: per_device(): lax.dot_general(columns, weighted, (((0,), (0,)), ((), ())), preferred_el...]
    unnamed x16 -> x19, local copies, waits for them, and re-layouts: 0.04 us -> 10.3 us
  transfers between devices with their start and end apart: 4 -> 0, of which waited for: 2 -> 0; matrix products, arithmetic and copies ran while one was open for 16% -> 0% of each run, Pallas kernels for 0% -> 0%
where the time goes in v1:
time: 94.3 us; the launch traced here: 93.9 us
  Pallas kernels  83 us (88%)
  local copies, waits for them, and re-layouts  10.3 us (11%)
    pallas_call x1, Pallas kernels, per_device(): pl.pallas_call(kernel, out_shape=[jax.ShapeDtypeStruct((rows, columns), F...  83 us
    unnamed x19, local copies, waits for them, and re-layouts  10.3 us

profile of v1, /device:TPU:1, one launch (start us, length us, event | category | flops | bytes accessed | tf_op | source)
XLA Modules:
  0.0 93.9 jit_solution(1105721978765272304)
XLA Ops:
  0.6 0.0 copy-start
  0.6 1.6 %copy-done = bf16[2048,512]{1,0:T(8,128)(2,1)S(1)} copy-done((bf16[2048,512]{1,0:T(8,128)(2,1)S(1)}, bf16[2048,512]{1,0:T(8,128)(2,1)}, u32[]{:S(2)}) %copy-start) | copy-done | bytes 2097176
  2.2 0.0 copy-start.1
  2.2 1.0 %copy-done.1 = bf16[256,1024]{1,0:T(8,128)(2,1)S(1)} copy-done((bf16[256,1024]{1,0:T(8,128)(2,1)S(1)}, bf16[256,1024]{1,0:T(8,128)(2,1)}, u32[]{:S(2)}) %copy-start.1) | copy-done | bytes 524312
  3.3 0.0 copy-start.2
  3.3 1.0 %copy-done.2 = bf16[1024,256]{1,0:T(8,128)(2,1)S(1)} copy-done((bf16[1024,256]{1,0:T(8,128)(2,1)S(1)}, bf16[1024,256]{1,0:T(8,128)(2,1)}, u32[]{:S(2)}) %copy-start.2) | copy-done | bytes 524312
  4.3 0.0 copy-start.3
  4.3 0.9 %copy-done.3 = s32[256,256]{1,0:T(8,128)S(1)} copy-done((s32[256,256]{1,0:T(8,128)S(1)}, s32[256,256]{1,0:T(8,128)}, u32[]{:S(2)}) %copy-start.3) | copy-done | bytes 262168
  5.3 0.0 copy-start.4
  5.3 0.9 %copy-done.4 = f32[128,512]{1,0:T(8,128)S(1)} copy-done((f32[128,512]{1,0:T(8,128)S(1)}, f32[128,512]{1,0:T(8,128)}, u32[]{:S(2)}) %copy-start.4) | copy-done | bytes 262168
  6.2 0.0 copy-start.5
  6.2 0.9 %copy-done.5 = f32[128,512]{1,0:T(8,128)S(1)} copy-done((f32[128,512]{1,0:T(8,128)S(1)}, f32[128,512]{1,0:T(8,128)}, u32[]{:S(2)}) %copy-start.5) | copy-done | bytes 262168
  7.2 0.0 copy-start.6
  7.2 0.9 %copy-done.6 = f32[128,512]{1,0:T(8,128)S(1)} copy-done((f32[128,512]{1,0:T(8,128)S(1)}, f32[128,512]{1,0:T(8,128)}, u32[]{:S(2)}) %copy-start.6) | copy-done | bytes 262168
  8.1 0.0 copy-start.7
  8.1 0.7 copy-done.7
  8.8 83.0 %shard_map.103 = (f32[128,512]{1,0:T(8,128)S(1)}, f32[128,512]{1,0:T(8,128)S(1)}, f32[128,512]{1,0:T(8,128)S(1)}) custom-call(s32[2,128]{1,0:T(2,128)S(1)} %bitcast.1, s32[256,256]{1,0:T(8,128)S(1)} %copy-done.3, bf16[2048,512]{1,0:T(8,128)(2,1)S(1)} %copy-done, f32[128,512]{1,0:T(8,128)S(1)} %copy-done.4, f32[128,512]{1,0:T(8,128)S(1)} %copy-done.5, ...), custom_call_target="tpu_custom_call" | custom-call | tf_op jit(solution)/shard_map/pallas_call | solution.py:430
  91.8 0.7 copy.14
  92.5 0.7 copy.15
  93.2 0.7 copy.16
Async XLA Ops:
  0.6 1.6 %copy-start = (bf16[2048,512]{1,0:T(8,128)(2,1)S(1)}, bf16[2048,512]{1,0:T(8,128)(2,1)}, u32[]{:S(2)}) copy-start(bf16[2048,512]{1,0:T(8,128)(2,1)} %weights_hbm.1) | copy-start | bytes 6291460
  2.2 1.0 %copy-start.1 = (bf16[256,1024]{1,0:T(8,128)(2,1)S(1)}, bf16[256,1024]{1,0:T(8,128)(2,1)}, u32[]{:S(2)}) copy-start(bf16[256,1024]{1,0:T(8,128)(2,1)} %constant.5.clone.lag_t_hbm) | copy-start | bytes 1572868
  3.3 1.0 %copy-start.2 = (bf16[1024,256]{1,0:T(8,128)(2,1)S(1)}, bf16[1024,256]{1,0:T(8,128)(2,1)}, u32[]{:S(2)}) copy-start(bf16[1024,256]{1,0:T(8,128)(2,1)} %constant.4.clone.lag_hbm) | copy-start | bytes 1572868
  4.3 0.9 %copy-start.3 = (s32[256,256]{1,0:T(8,128)S(1)}, s32[256,256]{1,0:T(8,128)}, u32[]{:S(2)}) copy-start(s32[256,256]{1,0:T(8,128)} %spikes_hbm.1) | copy-start | bytes 786436
  5.3 0.9 %copy-start.4 = (f32[128,512]{1,0:T(8,128)S(1)}, f32[128,512]{1,0:T(8,128)}, u32[]{:S(2)}) copy-start(f32[128,512]{1,0:T(8,128)} %direction_hbm.1) | copy-start | bytes 786436
  6.2 0.9 %copy-start.5 = (f32[128,512]{1,0:T(8,128)S(1)}, f32[128,512]{1,0:T(8,128)}, u32[]{:S(2)}) copy-start(f32[128,512]{1,0:T(8,128)} %residual_hbm.1) | copy-start | bytes 786436
  7.2 0.9 %copy-start.6 = (f32[128,512]{1,0:T(8,128)S(1)}, f32[128,512]{1,0:T(8,128)}, u32[]{:S(2)}) copy-start(f32[128,512]{1,0:T(8,128)} %iterate_hbm.1) | copy-start | bytes 786436
  8.1 0.7 copy-start.7

commit v2 on v1

--- a/solution.py
+++ b/solution.py
@@ -51,9 +51,9 @@
 
 
 def kernel(
-    exposure_ref, spikes_hbm, weights_hbm, direction_hbm, residual_hbm, iterate_hbm, lag_hbm, lag_t_hbm,
-    iterate_out, residual_out, direction_out,
-    spikes_in, lag, lag_t, d32, r32, it32, w16, w32, wp, spk, spk_t, x, xt,
+    exposure_ref, spikes_hbm, weights_hbm, direction_hbm, residual_hbm, lag_hbm, lag_t_hbm,
+    product_out, step_out, ratio_out,
+    spikes_in, lag, lag_t, d32, r32, w16, w32, wp, spk, spk_t, x, xt,
     d_send, d_all, p_own, p_send, p_recv, a_own, a_send, a_recv, wt_all, g_send, g_recv, g_nat,
     ticks, ticks_t, nd_send, nd_recv, cv_send, cv_recv, c2_send, c2_recv, nn_send, nn_recv, nz_send, nz_recv,
     load_sem, spk_sem, halo_sem, tick_sem, d_sem, p_sem, a_sem, wt_sem, g_sem, nd_sem, cv_sem, c2_sem, nn_sem, nz_sem,
@@ -99,11 +99,11 @@
             pltpu.make_async_copy(source.at[:, k * COLS : (k + 1) * COLS], target.at[k], load_sem.at[4 + 4 * n + k])
             for k in range(GROUP)
         ]
-        for n, (source, target) in enumerate(((direction_hbm, d32), (residual_hbm, r32), (iterate_hbm, it32)))
+        for n, (source, target) in enumerate(((direction_hbm, d32), (residual_hbm, r32)))
     ]
     for copy in blocks[0] + loads[:1]:
         copy.start()
-    for copy in loads[1:] + blocks[1] + blocks[2]:
+    for copy in loads[1:] + blocks[1]:
         copy.start()
 
     barrier = pltpu.get_barrier_semaphore()
@@ -289,18 +289,26 @@
     def gram_copy(step):
         return remote(g_send.at[tm_peer(step)], g_recv.at[me], g_sem, step, tm_peer(step), z)
 
+    def gram_to(peer):
+        return remote(g_send.at[peer], g_recv.at[me], g_sem, lax.rem(peer + TM - me, TM), peer, z)
+
     def gram_arrival(step):
         return remote(g_send.at[0], g_recv.at[tm_peer(TM - step)], g_sem, step, tm_peer(step), z)
 
-    def gram(slots):
-        rows = pl.ds(slots * 4, 4)
+    def gram(turn):
+        group = lax.rem(team + turn, GROUP)
+        rows = pl.ds(group * 4, 4)
         made = jnp.dot(
             xt[rows].reshape(4 * SLOT * BASES, BINS), wt_all[...].reshape(BINS, COLS), preferred_element_type=F32
         )
         g_send[rows] = made.astype(BF16).reshape(4, SLOT * BASES, COLS)
 
-    each(0, 4, gram)
-    each(1, TM, lambda step: gram_copy(step).start())
+        @pl.when(turn < 4)
+        def _():
+            each(0, GROUP, lambda k: gram_to(group * GROUP + k).start())
+
+    each(1, 5, gram)
+    each(1, GROUP, lambda step: gram_to(team_peer(step)).start())
     g_recv[me] = g_send[me]
 
     each(1, NIN, lambda step: cv_copy(step).wait_recv())
@@ -317,8 +325,6 @@
 
     each(1, TM, lambda step: c2_copy(step).start())
     each(1, TM, lambda step: c2_arrival(step).wait_recv())
-    for copy in blocks[2]:
-        copy.wait()
     step_sizes = []
     for k in range(GROUP):
         total = c2_recv[k, 0:1, :]
@@ -327,7 +333,7 @@
         curvature = total / (BINS * (TM // GROUP)) + RIDGE_WEIGHT * cv_sum[4 + k : 5 + k, :]
         step_size = old_norm[k : k + 1, :] / curvature
         step_sizes.append(step_size)
-        iterate_out[:, k * COLS : (k + 1) * COLS] = it32[k] + step_size * d32[k]
+        step_out[:, k * COLS : (k + 1) * COLS] = step_size
 
     each(1, TM, lambda step: gram_arrival(step).wait_recv())
     nn_send[4:8, :] = jnp.zeros((4, COLS), F32)
@@ -339,7 +345,7 @@
             g_nat[k, pl.ds(b, SLOT, stride=BASES), :] = total[b * SLOT : (b + 1) * SLOT]
         product = g_nat[k] / (BINS * (TM // GROUP)) + RIDGE_WEIGHT * d32[k]
         new_residual = r32[k] - step_sizes[k] * product
-        residual_out[:, k * COLS : (k + 1) * COLS] = new_residual
+        product_out[:, k * COLS : (k + 1) * COLS] = product
         nn_send[k : k + 1, :] = jnp.sum(new_residual * new_residual, axis=0, keepdims=True)
 
     def nn_copy(step):
@@ -356,9 +362,8 @@
     each(1, NIN, lambda step: nz_copy(step).wait_recv())
     new_norm = nz_send[...] + jnp.sum(nz_recv[1:NIN], axis=0)
     for k in range(GROUP):
-        columns = slice(k * COLS, (k + 1) * COLS)
         ratio = new_norm[k : k + 1, :] / (old_norm[k : k + 1, :] + NORM_EPS)
-        direction_out[:, columns] = residual_out[:, columns] + ratio * d32[k]
+        ratio_out[:, k * COLS : (k + 1) * COLS] = ratio
 
     each(1, GROUP, lambda step: spikes_copy(step).wait_send())
 
@@ -388,7 +393,6 @@
         pltpu.VMEM((OWN, NEUR), jnp.int32),
         pltpu.VMEM((BASES * HISTORY, 2 * HISTORY), BF16),
         pltpu.VMEM((2 * HISTORY, BASES * HISTORY), BF16),
-        pltpu.VMEM((GROUP, rows, COLS), F32),
         pltpu.VMEM((GROUP, rows, COLS), F32),
         pltpu.VMEM((GROUP, rows, COLS), F32),
         pltpu.VMEM((FEAT, COLS), BF16),
@@ -427,16 +431,18 @@
         pair(TM), pair(NIN), pair(2 * NIN), pair(2 * NIN), pair(TM),
         pair(TM), pair(NIN), pair(TM), pair(TM), pair(NIN),
     ]
-    return pl.pallas_call(
+    product, step_size, ratio = pl.pallas_call(
         kernel,
-        out_shape=[jax.ShapeDtypeStruct((rows, columns), F32)] * 3,
-        in_specs=[vmem] + [hbm] * 7,
+        out_shape=[jax.ShapeDtypeStruct((rows, columns), F32), *[jax.ShapeDtypeStruct((1, columns), F32)] * 2],
+        in_specs=[vmem] + [hbm] * 6,
         out_specs=[vmem] * 3,
         scratch_shapes=scratch,
         compiler_params=pltpu.CompilerParams(
-            collective_id=0, has_side_effects=True, vmem_limit_bytes=40 * 2**20
+            collective_id=0, has_side_effects=True, vmem_limit_bytes=60 * 2**20
         ),
-    )(exposure.reshape(2, COLS), spikes, weights, direction, residual, iterate, lag, lag_t)
+    )(exposure.reshape(2, COLS), spikes, weights, direction, residual, lag, lag_t)
+    new_residual = residual - step_size * product
+    return iterate + step_size * direction, new_residual, new_residual + ratio * direction
 
 
 def solution(mesh):

time: 94.3 us -> 85.4 us (0.906)
  local copies, waits for them, and re-layouts: 10.3 us -> 0.01 us
  other arithmetic: 0 us -> 1.92 us
    unnamed x19 -> x6, local copies, waits for them, and re-layouts: 10.3 us -> 0.01 us
    add x0 -> x1, other arithmetic: none -> 1.92 us  [per_device(): new_residual + ratio * direction]
where the time goes in v2:
time: 85.4 us; the launch traced here: 85.2 us
  Pallas kernels  82.6 us (97%)
  other arithmetic  1.92 us (2%)
    pallas_call x1, Pallas kernels, per_device(): pl.pallas_call(kernel, out_shape=[jax.ShapeDtypeStruct((rows, columns), F...  82.6 us
    add x1, other arithmetic, per_device(): new_residual + ratio * direction  1.92 us

profile of v2, /device:TPU:1, one launch (start us, length us, event | category | flops | bytes accessed | tf_op | source)
XLA Modules:
  0.0 85.2 jit_solution(2542926102250319885)
XLA Ops:
  0.6 0.0 copy-start.1
  0.6 0.0 copy-start
  0.7 0.0 copy-start.2
  0.7 82.6 %shard_map.103 = (f32[128,512]{1,0:T(8,128)}, f32[1,512]{1,0:T(1,128)}, f32[1,512]{1,0:T(1,128)}) custom-call(s32[2,128]{1,0:T(2,128)} %bitcast.5, s32[256,256]{1,0:T(8,128)} %spikes_hbm.1, bf16[2048,512]{1,0:T(8,128)(2,1)} %weights_hbm.1, f32[128,512]{1,0:T(8,128)} %direction_hbm.1, f32[128,512]{1,0:T(8,128)} %residual_hbm.1, ...), custom_call_target="tpu_custom_call" | custom-call | tf_op jit(solution)/shard_map/pallas_call | solution.py:434
  83.3 0.0 copy-done.1
  83.3 0.0 copy-done
  83.3 0.0 copy-done.2
  83.3 1.9 %multiply_add_fusion = (f32[128,512]{1,0:T(8,128)}, f32[128,512]{1,0:T(8,128)}, f32[128,512]{1,0:T(8,128)}) fusion(f32[128,512]{1,0:T(8,128)S(1)} %copy-done, f32[512]{0:T(512)} %bitcast.4, f32[128,512]{1,0:T(8,128)S(1)} %copy-done.1, f32[128,512]{1,0:T(8,128)} %get-tuple-element.7, f32[512]{0:T(512)} %bitcast.3, f32[128,512]{1,0:T(8,128)S(1)} %copy-done.2), kind=kLoop, calls=%fused_computation | loop fusion | flops 393216 | bytes 1839104 | tf_op jit(solution)/shard_map/add | solution.py:445
Async XLA Ops:
  0.6 82.6 %copy-start.1 = (f32[128,512]{1,0:T(8,128)S(1)}, f32[128,512]{1,0:T(8,128)}, u32[]{:S(2)}) copy-start(f32[128,512]{1,0:T(8,128)} %residual_hbm.1) | copy-start | bytes 786436
  0.6 82.6 %copy-start = (f32[128,512]{1,0:T(8,128)S(1)}, f32[128,512]{1,0:T(8,128)}, u32[]{:S(2)}) copy-start(f32[128,512]{1,0:T(8,128)} %direction_hbm.1) | copy-start | bytes 786436
  0.7 82.6 %copy-start.2 = (f32[128,512]{1,0:T(8,128)S(1)}, f32[128,512]{1,0:T(8,128)}, u32[]{:S(2)}) copy-start(f32[128,512]{1,0:T(8,128)} %param.13) | copy-start | bytes 786436

commit v3 on v2

--- a/solution.py
+++ b/solution.py
@@ -19,6 +19,8 @@
 
 TM = 16
 NIN = 8
+NOUT = 4
+EARLY = 3
 GROUP = 4
 BINS = 1024
 OWN = 256
@@ -73,11 +75,25 @@
     def team_peer(step):
         return team * GROUP + lax.rem(part + step, GROUP)
 
-    def remote(src, dst, sems, slot, tm_index, z_index):
+    chip = me // 2
+    core = lax.rem(me, 2)
+    half_own = lax.rem(chip, 2)
+    mate = chip + 1 - 2 * half_own
+
+    def x_peer(step):
+        return lax.rem(xo + step, NOUT)
+
+    def swing(turn, middle):
+        return middle + (1 - 2 * lax.rem(turn, 2)) * ((turn + 1) // 2)
+
+    def remote(src, dst, sems, slot, tm_index, z_index, x_index=None):
         return pltpu.make_async_remote_copy(
             src_ref=src, dst_ref=dst, send_sem=sems.at[0, slot], recv_sem=sems.at[1, slot],
-            device_id=(tm_index, z_index, xo), device_id_type=MESH,
+            device_id=(tm_index, z_index, xo if x_index is None else x_index), device_id_type=MESH,
         )
+
+    def far_first(count, body):
+        each(0, count - 1, lambda turn: body(swing(turn, count // 2)))
 
     def each(first, last, body):
         def run(step, carry):
@@ -117,6 +133,14 @@
     each(1, TM, greet_tm)
     each(1, NIN, greet_z)
 
+    def greet_x(step):
+        for c in range(2):
+            pl.semaphore_signal(
+                barrier, inc=1, device_id=(chip * 2 + c, z, x_peer(step)), device_id_type=MESH
+            )
+
+    each(1, NOUT, greet_x)
+
     for copy in blocks[0]:
         copy.wait()
     for k in range(GROUP):
@@ -127,19 +151,52 @@
     spk[own_rows, :] = spikes_in[...].astype(F32).astype(BF16)
     ticks[part, 0:2, :] = exposure_ref[...].astype(F32) / 8.0
     ticks[part, 2:8, :] = jnp.zeros((6, COLS), F32)
-    pl.semaphore_wait(barrier, TM - 1 + NIN - 1)
-
-    def spikes_copy(step):
-        return remote(spk.at[own_rows], spk.at[own_rows], spk_sem, step, team_peer(step), z)
-
-    def spikes_arrival(step):
-        rows = pl.ds(pl.multiple_of(HISTORY + lax.rem(part + GROUP - step, GROUP) * OWN, HISTORY), OWN)
-        return remote(spk.at[rows], spk.at[rows], spk_sem, step, team_peer(step), z)
+    pl.semaphore_wait(barrier, TM - 1 + NIN - 1 + 2 * (NOUT - 1))
+
+    def core_copy():
+        return remote(spk.at[own_rows], spk.at[own_rows], spk_sem, 8, chip * 2 + 1 - core, z)
+
+    def core_arrival():
+        rows = pl.ds(pl.multiple_of(HISTORY + (half_own * 2 + 1 - core) * OWN, HISTORY), OWN)
+        return remote(spk.at[rows], spk.at[rows], spk_sem, 8, chip * 2 + 1 - core, z)
+
+    def quarter(half, from_core, x_index):
+        return pl.ds(pl.multiple_of(HISTORY + (half * 2 + from_core) * OWN + x_index * 64, 64), 64)
+
+    def mate_copy():
+        rows = quarter(half_own, core, xo)
+        return remote(spk.at[rows], spk.at[rows], spk_sem, 0, mate * 2 + core, z)
+
+    def mate_arrival(step, other):
+        from_core = core if other == 0 else 1 - core
+        rows = quarter(1 - half_own, from_core, x_peer(NOUT - step))
+        return remote(spk.at[rows], spk.at[rows], spk_sem, step * 2 + other, me, z)
+
+    def spread_copy(step, other):
+        rows = quarter(1 - half_own, core, xo)
+        to_core = core if other == 0 else 1 - core
+        return remote(spk.at[rows], spk.at[rows], spk_sem, step * 2 + other, chip * 2 + to_core, z, x_peer(step))
 
     def halo_copy(k):
+        rows = pl.ds(pl.multiple_of(BINS + xo * 32, 32), 32)
         return remote(
-            spk.at[BINS : BINS + HISTORY], spk.at[0:HISTORY], halo_sem, k, lax.rem((team + 1) * GROUP + k, TM), z
+            spk.at[rows], spk.at[halo_rows(xo)], halo_sem, 8 + k, lax.rem((team + 1) * GROUP + 2 * k + 1, TM), z
         )
+
+    def halo_rows(x_index):
+        return pl.ds(pl.multiple_of(x_index * 32, 32), 32)
+
+    def halo_first():
+        rows = halo_rows(xo)
+        return remote(spk.at[rows], spk.at[rows], halo_sem, 8 + half_own, me, z)
+
+    def halo_spread(step, other):
+        rows = halo_rows(xo)
+        return remote(spk.at[rows], spk.at[rows], halo_sem, step * 2 + other, chip * 2 + 1 - other, z, x_peer(step))
+
+    def halo_arrival(step):
+        rows = halo_rows(x_peer(NOUT - step))
+        return remote(spk.at[rows], spk.at[rows], halo_sem, step * 2 + 1 - core, me, z)
 
     def tick_copy(step):
         return remote(ticks.at[part], ticks.at[part], tick_sem, step, team_peer(step), z)
@@ -159,53 +216,35 @@
         return remote(d_send.at[0], d_all.at[:, rows, :], d_sem, step, tm_peer(step), z)
 
     sends_halo = jnp.logical_and(part == GROUP - 1, team < TM // GROUP - 1)
-
-    each(1, GROUP, lambda step: spikes_copy(step).start())
+    hands_halo = jnp.logical_and(core == 1, team > 0)
+    spreads = [(step, other) for step in (2, 1, 3, 0) for other in range(2) if (step, other) != (0, 0)]
+
+    mate_copy().start()
 
     @pl.when(sends_halo)
     def _():
-        each(0, GROUP, lambda k: halo_copy(k).start())
-
-    each(1, TM, lambda step: direction_copy(step).start())
+        halo_copy(0).start()
+        halo_copy(1).start()
+
+    core_copy().start()
+    far_first(TM, lambda step: direction_copy(step).start())
     each(1, GROUP, lambda step: tick_copy(step).start())
     d_all[:, d_rows, :] = d_send[part]
-
-    for copy in blocks[1]:
-        copy.wait()
-    for k in range(GROUP):
-        nd_send[k : k + 1, :] = jnp.sum(r32[k] * r32[k], axis=0, keepdims=True)
-        nd_send[GROUP + k : GROUP + k + 1, :] = jnp.sum(d32[k] * d32[k], axis=0, keepdims=True)
-
-    def nd_copy(step):
-        return remote(nd_send, nd_recv.at[step], nd_sem, step, tm_peer(step), z)
-
-    each(1, TM, lambda step: nd_copy(step).start())
 
     loads[3].wait()
     w32[...] = w16[...].astype(F32)
     for b in range(BASES):
         wp[b * NEUR : (b + 1) * NEUR, :] = w32[pl.ds(b, NEUR, stride=BASES), :].astype(BF16)
-    loads[1].wait()
-    loads[2].wait()
-
-    @pl.when(team == 0)
-    def _():
-        spk[0:HISTORY, :] = jnp.zeros((HISTORY, NEUR), BF16)
-
-    @pl.when(team > 0)
-    def _():
-        pltpu.make_async_remote_copy(
-            src_ref=spk.at[0:HISTORY], dst_ref=spk.at[0:HISTORY], send_sem=halo_sem.at[0, part],
-            recv_sem=halo_sem.at[1, part], device_id=(me, z, xo), device_id_type=MESH,
-        ).wait_recv()
-
-    each(1, GROUP, lambda step: spikes_arrival(step).wait_recv())
-
-    for n in range(9):
-        spk_t[:, n * HISTORY : (n + 1) * HISTORY] = spk[n * HISTORY : (n + 1) * HISTORY, :].astype(F32).T.astype(BF16)
-
-    def features(block):
-        rows = pl.ds(pl.multiple_of(block * HISTORY, HISTORY), HISTORY)
+
+    def turn_spikes(n):
+        rows = pl.ds(pl.multiple_of(n * HISTORY, HISTORY), HISTORY)
+        spk_t[:, rows] = spk[rows, :].astype(F32).T.astype(BF16)
+
+    own_first = half_own * 4 + 1
+
+    def features(k):
+        block = lax.rem(own_first + k, 8)
+        rows = pl.ds(pl.multiple_of(k * HISTORY, HISTORY), HISTORY)
         window = pl.ds(pl.multiple_of(block * HISTORY, HISTORY), 2 * HISTORY)
         made = jnp.dot(lag[...], spk[window, :], preferred_element_type=F32)
         for b in range(BASES):
@@ -215,63 +254,110 @@
             piece = made_t[:, b * HISTORY : (b + 1) * HISTORY].astype(BF16)
             xt[:, b, :, rows] = piece.reshape(TM, SLOT, HISTORY)
 
-    each(0, BINS // HISTORY, features)
-
-    def predictor(half):
-        rows = pl.ds(pl.multiple_of(half * 512, 512), 512)
-        made = jnp.dot(x[rows, :], wp[...], preferred_element_type=F32).reshape(NIN, 64, COLS)
-        p_own[half] = made
-        p_send[half] = made.astype(BF16)
-
-    each(0, 2, predictor)
-
-    def predictor_copy(step):
-        return remote(p_send.at[:, z_peer(step)], p_recv.at[:, step], p_sem, step, me, z_peer(step))
-
-    each(1, NIN, lambda step: predictor_copy(step).start())
+    loads[1].wait()
+    loads[2].wait()
+    core_arrival().wait_recv()
+    each(0, 4, lambda k: turn_spikes(own_first + k))
+    each(0, EARLY, features)
+
+    mate_arrival(0, 0).wait_recv()
+    for step, other in spreads:
+        spread_copy(step, other).start()
+
+    @pl.when(team == 0)
+    def _():
+        spk[0:HISTORY, :] = jnp.zeros((HISTORY, NEUR), BF16)
+
+    @pl.when(hands_halo)
+    def _():
+        halo_first().wait_recv()
+        for step, other in spreads:
+            halo_spread(step, other).start()
+
+    def predictor(first, last):
+        made = jnp.dot(x[first * HISTORY : last * HISTORY, :], wp[...], preferred_element_type=F32)
+        made = made.reshape(last - first, NIN, 16, COLS)
+        p_own[first:last] = made
+        p_send[first:last] = made.astype(BF16)
+
+    def predictor_copy(late, step):
+        blocks_of = slice(EARLY, 8) if late else slice(0, EARLY)
+        return remote(
+            p_send.at[blocks_of, z_peer(step)], p_recv.at[blocks_of, step], p_sem, late * NIN + step, me, z_peer(step)
+        )
+
+    predictor(0, EARLY)
+    far_first(NIN, lambda step: predictor_copy(0, step).start())
+
+    for copy in blocks[1]:
+        copy.wait()
+    for k in range(GROUP):
+        nd_send[k : k + 1, :] = jnp.sum(r32[k] * r32[k], axis=0, keepdims=True)
+        nd_send[GROUP + k : GROUP + k + 1, :] = jnp.sum(d32[k] * d32[k], axis=0, keepdims=True)
+
+    def nd_copy(step):
+        return remote(nd_send, nd_recv.at[step], nd_sem, step, tm_peer(step), z)
+
+    each(1, TM, lambda step: nd_copy(step).start())
+
+    for step, other in spreads:
+        mate_arrival(step, other).wait_recv()
+
+    @pl.when(team > 0)
+    def _():
+        each(core, NOUT, lambda step: halo_arrival(step).wait_recv())
+
+    each(0, 5, lambda k: turn_spikes(lax.rem(own_first + 4 + k, 9)))
+    each(EARLY, 8, features)
+    predictor(EARLY, 8)
+    far_first(NIN, lambda step: predictor_copy(1, step).start())
 
     each(1, TM, lambda step: direction_arrival(step).wait_recv())
 
     def along_copy(half, step):
-        return remote(a_send.at[half, z_peer(step)], a_recv.at[half, step], a_sem, half * NIN + step, me, z_peer(step))
-
-    def along(half):
-        rows = pl.ds(pl.multiple_of(half * 512, 512), 512)
-        made = jnp.dot(x[rows, :], d_all[...].reshape(FEAT, COLS), preferred_element_type=F32).reshape(NIN, 64, COLS)
-        a_own[half] = made
-        a_send[half] = made.astype(BF16)
-        each(1, NIN, lambda step: along_copy(half, step).start())
-
-    each(0, 2, along)
+        blocks_of = slice(half * 4, half * 4 + 4)
+        return remote(
+            a_send.at[blocks_of, z_peer(step)], a_recv.at[blocks_of, step], a_sem, half * NIN + step, me, z_peer(step)
+        )
+
+    for half in range(2):
+        made = jnp.dot(
+            x[half * 512 : half * 512 + 512, :], d_all[...].reshape(FEAT, COLS), preferred_element_type=F32
+        ).reshape(4, NIN, 16, COLS)
+        a_own[half * 4 : half * 4 + 4] = made
+        a_send[half * 4 : half * 4 + 4] = made.astype(BF16)
+        far_first(NIN, lambda step: along_copy(half, step).start())
 
     each(1, GROUP, lambda step: tick_arrival(step).wait_recv())
     table = jnp.concatenate([ticks[k, 0:2, :] for k in range(GROUP)] + [jnp.zeros((COLS - 8, COLS), F32)], axis=0)
     ticks_t[...] = table.T
-    tick_rows = ticks_t[pl.ds(pl.multiple_of(lax.rem(z, 2) * 64, 64), 64), :]
-    lane = lax.broadcasted_iota(jnp.int32, (64, COLS), 1)
+    tick_rows = ticks_t[pl.ds(pl.multiple_of(z * 16, 16), 16), :]
+    lane = lax.broadcasted_iota(jnp.int32, (16, COLS), 1)
 
     each(1, TM, lambda step: nd_copy(step).wait_recv())
     cv_send[0:8, :] = nd_send[...] + jnp.sum(nd_recv[1:TM], axis=0)
 
-    each(1, NIN, lambda step: predictor_copy(step).wait_recv())
+    for late in range(2):
+        each(1, NIN, lambda step: predictor_copy(late, step).wait_recv())
+
+    def weighted_copy(half, slot, step):
+        place = wt_all.at[slice(half * 4, half * 4 + 4), slot]
+        return remote(place, place, wt_sem, half * NIN + step, me, z_peer(step))
+
     curvature_part = jnp.zeros((1, COLS), F32)
     for half in range(2):
         each(1, NIN, lambda step: along_copy(half, step).wait_recv())
-        p_sum = p_own[half, z]
-        a_sum = a_own[half, z]
-        for step in range(1, NIN):
-            p_sum += p_recv[half, step].astype(F32)
-            a_sum += a_recv[half, step].astype(F32)
-        scale = jnp.sum(jnp.where(lane == half * 4 + z // 2, tick_rows, 0.0), axis=1, keepdims=True)
-        weighted = ((scale * jnp.exp(p_sum)) * a_sum).astype(BF16)
-        wt_all[half, z] = weighted
-        each(
-            1, NIN,
-            lambda step: remote(
-                wt_all.at[half, z], wt_all.at[half, z], wt_sem, half * NIN + step, me, z_peer(step)
-            ).start(),
-        )
-        curvature_part += jnp.sum(weighted.astype(F32) * a_sum, axis=0, keepdims=True)
+        for k in range(half * 4, half * 4 + 4):
+            p_sum = p_own[k, z]
+            a_sum = a_own[k, z]
+            for step in range(1, NIN):
+                p_sum += p_recv[k, step].astype(F32)
+                a_sum += a_recv[k, step].astype(F32)
+            scale = jnp.sum(jnp.where(lane == lax.rem(own_first + k, 8), tick_rows, 0.0), axis=1, keepdims=True)
+            weighted = ((scale * jnp.exp(p_sum)) * a_sum).astype(BF16)
+            wt_all[k, z] = weighted
+            curvature_part += jnp.sum(weighted.astype(F32) * a_sum, axis=0, keepdims=True)
+        far_first(NIN, lambda step: weighted_copy(half, z, step).start())
     cv_send[8:16, :] = jnp.concatenate([curvature_part, jnp.zeros((7, COLS), F32)], axis=0)
 
     def cv_copy(step):
@@ -279,12 +365,8 @@
 
     each(1, NIN, lambda step: cv_copy(step).start())
 
-    def weighted_arrival(half, step):
-        slot = z_peer(NIN - step)
-        return remote(wt_all.at[half, slot], wt_all.at[half, slot], wt_sem, half * NIN + step, me, z_peer(step))
-
     for half in range(2):
-        each(1, NIN, lambda step: weighted_arrival(half, step).wait_recv())
+        each(1, NIN, lambda step: weighted_copy(half, z_peer(NIN - step), step).wait_recv())
 
     def gram_copy(step):
         return remote(g_send.at[tm_peer(step)], g_recv.at[me], g_sem, step, tm_peer(step), z)
@@ -296,18 +378,18 @@
         return remote(g_send.at[0], g_recv.at[tm_peer(TM - step)], g_sem, step, tm_peer(step), z)
 
     def gram(turn):
-        group = lax.rem(team + turn, GROUP)
+        group = lax.rem(team + swing(turn, 2), GROUP)
         rows = pl.ds(group * 4, 4)
         made = jnp.dot(
             xt[rows].reshape(4 * SLOT * BASES, BINS), wt_all[...].reshape(BINS, COLS), preferred_element_type=F32
         )
         g_send[rows] = made.astype(BF16).reshape(4, SLOT * BASES, COLS)
 
-        @pl.when(turn < 4)
+        @pl.when(turn < 3)
         def _():
             each(0, GROUP, lambda k: gram_to(group * GROUP + k).start())
 
-    each(1, 5, gram)
+    each(0, 4, gram)
     each(1, GROUP, lambda step: gram_to(team_peer(step)).start())
     g_recv[me] = g_send[me]
 
@@ -351,34 +433,44 @@
     def nn_copy(step):
         return remote(nn_send, nn_recv.at[step], nn_sem, step, tm_peer(step), z)
 
-    each(1, TM, lambda step: nn_copy(step).start())
+    far_first(TM, lambda step: nn_copy(step).start())
     each(1, TM, lambda step: nn_copy(step).wait_recv())
     nz_send[...] = nn_send[...] + jnp.sum(nn_recv[1:TM], axis=0)
 
     def nz_copy(step):
         return remote(nz_send, nz_recv.at[step], nz_sem, step, me, z_peer(step))
 
-    each(1, NIN, lambda step: nz_copy(step).start())
+    far_first(NIN, lambda step: nz_copy(step).start())
     each(1, NIN, lambda step: nz_copy(step).wait_recv())
     new_norm = nz_send[...] + jnp.sum(nz_recv[1:NIN], axis=0)
     for k in range(GROUP):
         ratio = new_norm[k : k + 1, :] / (old_norm[k : k + 1, :] + NORM_EPS)
         ratio_out[:, k * COLS : (k + 1) * COLS] = ratio
 
-    each(1, GROUP, lambda step: spikes_copy(step).wait_send())
+    mate_copy().wait_send()
+    core_copy().wait_send()
+    for step, other in spreads:
+        spread_copy(step, other).wait_send()
 
     @pl.when(sends_halo)
     def _():
-        each(0, GROUP, lambda k: halo_copy(k).wait_send())
+        halo_copy(0).wait_send()
+        halo_copy(1).wait_send()
+
+    @pl.when(hands_halo)
+    def _():
+        for step, other in spreads:
+            halo_spread(step, other).wait_send()
 
     each(1, GROUP, lambda step: tick_copy(step).wait_send())
     for copy in (direction_copy, nd_copy, gram_copy, c2_copy, nn_copy):
         each(1, TM, lambda step: copy(step).wait_send())
-    for copy in (predictor_copy, cv_copy, nz_copy):
+    for copy in (cv_copy, nz_copy):
         each(1, NIN, lambda step: copy(step).wait_send())
     for half in range(2):
         each(1, NIN, lambda step: along_copy(half, step).wait_send())
-        each(1, NIN, lambda step: weighted_arrival(half, step).wait_send())
+        each(1, NIN, lambda step: weighted_copy(half, z, step).wait_send())
+        each(1, NIN, lambda step: predictor_copy(half, step).wait_send())
 
 
 def per_device(spikes, exposure, weights, direction, residual, iterate):
@@ -404,13 +496,13 @@
         pltpu.VMEM((TM, BASES, SLOT, BINS), BF16),
         pltpu.VMEM((GROUP, BASES, SLOT, COLS), BF16),
         pltpu.VMEM((BASES, NEUR, COLS), BF16),
-        pltpu.VMEM((2, NIN, 64, COLS), F32),
-        pltpu.VMEM((2, NIN, 64, COLS), BF16),
-        pltpu.VMEM((2, NIN, 64, COLS), BF16),
-        pltpu.VMEM((2, NIN, 64, COLS), F32),
-        pltpu.VMEM((2, NIN, 64, COLS), BF16),
-        pltpu.VMEM((2, NIN, 64, COLS), BF16),
-        pltpu.VMEM((2, NIN, 64, COLS), BF16),
+        pltpu.VMEM((8, NIN, 16, COLS), F32),
+        pltpu.VMEM((8, NIN, 16, COLS), BF16),
+        pltpu.VMEM((8, NIN, 16, COLS), BF16),
+        pltpu.VMEM((8, NIN, 16, COLS), F32),
+        pltpu.VMEM((8, NIN, 16, COLS), BF16),
+        pltpu.VMEM((8, NIN, 16, COLS), BF16),
+        pltpu.VMEM((8, NIN, 16, COLS), BF16),
         pltpu.VMEM((TM, rows, COLS), BF16),
         pltpu.VMEM((TM, rows, COLS), BF16),
         pltpu.VMEM((GROUP, rows, COLS), F32),
@@ -427,8 +519,8 @@
         pltpu.VMEM((8, COLS), F32),
         pltpu.VMEM((NIN, 8, COLS), F32),
         pltpu.SemaphoreType.DMA((16,)),
-        pair(GROUP), pair(GROUP), pair(GROUP),
-        pair(TM), pair(NIN), pair(2 * NIN), pair(2 * NIN), pair(TM),
+        pair(9), pair(10), pair(GROUP),
+        pair(TM), pair(2 * NIN), pair(2 * NIN), pair(2 * NIN), pair(TM),
         pair(TM), pair(NIN), pair(TM), pair(TM), pair(NIN),
     ]
     product, step_size, ratio = pl.pallas_call(

time: 85.4 us -> 81.6 us (0.956)
  Pallas kernels: 82.6 us -> 78.8 us
    pallas_call x1, Pallas kernels: 82.6 us -> 78.8 us  [per_device(): pl.pallas_call(kernel, out_shape=[jax.ShapeDtypeStruct((rows, columns), F...]
where the time goes in v3:
time: 81.6 us; the launch traced here: 81.4 us
  Pallas kernels  78.8 us (97%)
  other arithmetic  1.92 us (2%)
    pallas_call x1, Pallas kernels, per_device(): pl.pallas_call(kernel, out_shape=[jax.ShapeDtypeStruct((rows, columns), F...  78.8 us
    add x1, other arithmetic, per_device(): new_residual + ratio * direction  1.92 us

profile of v3, /device:TPU:1, one launch (start us, length us, event | category | flops | bytes accessed | tf_op | source)
XLA Modules:
  0.0 81.4 jit_solution(8914600853567176032)
XLA Ops:
  0.6 0.0 copy-start.1
  0.6 0.0 copy-start
  0.7 0.0 copy-start.2
  0.7 78.8 %shard_map.103 = (f32[128,512]{1,0:T(8,128)}, f32[1,512]{1,0:T(1,128)}, f32[1,512]{1,0:T(1,128)}) custom-call(s32[2,128]{1,0:T(2,128)} %bitcast.5, s32[256,256]{1,0:T(8,128)} %spikes_hbm.1, bf16[2048,512]{1,0:T(8,128)(2,1)} %weights_hbm.1, f32[128,512]{1,0:T(8,128)} %direction_hbm.1, f32[128,512]{1,0:T(8,128)} %residual_hbm.1, ...), custom_call_target="tpu_custom_call" | custom-call | tf_op jit(solution)/shard_map/pallas_call | solution.py:526
  79.5 0.0 copy-done.1
  79.5 0.0 copy-done
  79.5 0.0 copy-done.2
  79.5 1.9 %multiply_add_fusion = (f32[128,512]{1,0:T(8,128)}, f32[128,512]{1,0:T(8,128)}, f32[128,512]{1,0:T(8,128)}) fusion(f32[128,512]{1,0:T(8,128)S(1)} %copy-done, f32[512]{0:T(512)} %bitcast.4, f32[128,512]{1,0:T(8,128)S(1)} %copy-done.1, f32[128,512]{1,0:T(8,128)} %get-tuple-element.7, f32[512]{0:T(512)} %bitcast.3, f32[128,512]{1,0:T(8,128)S(1)} %copy-done.2), kind=kLoop, calls=%fused_computation | loop fusion | flops 393216 | bytes 1839104 | tf_op jit(solution)/shard_map/add | solution.py:537
Async XLA Ops:
  0.6 78.8 %copy-start.1 = (f32[128,512]{1,0:T(8,128)S(1)}, f32[128,512]{1,0:T(8,128)}, u32[]{:S(2)}) copy-start(f32[128,512]{1,0:T(8,128)} %residual_hbm.1) | copy-start | bytes 786436
  0.6 78.8 %copy-start = (f32[128,512]{1,0:T(8,128)S(1)}, f32[128,512]{1,0:T(8,128)}, u32[]{:S(2)}) copy-start(f32[128,512]{1,0:T(8,128)} %direction_hbm.1) | copy-start | bytes 786436
  0.7 78.8 %copy-start.2 = (f32[128,512]{1,0:T(8,128)S(1)}, f32[128,512]{1,0:T(8,128)}, u32[]{:S(2)}) copy-start(f32[128,512]{1,0:T(8,128)} %param.13) | copy-start | bytes 786436

commit v4 on v3

--- a/solution.py
+++ b/solution.py
@@ -58,7 +58,7 @@
     spikes_in, lag, lag_t, d32, r32, w16, w32, wp, spk, spk_t, x, xt,
     d_send, d_all, p_own, p_send, p_recv, a_own, a_send, a_recv, wt_all, g_send, g_recv, g_nat,
     ticks, ticks_t, nd_send, nd_recv, cv_send, cv_recv, c2_send, c2_recv, nn_send, nn_recv, nz_send, nz_recv,
-    load_sem, spk_sem, halo_sem, tick_sem, d_sem, p_sem, a_sem, wt_sem, g_sem, nd_sem, cv_sem, c2_sem, nn_sem, nz_sem,
+    load_sem, on_sem, spk_sem, halo_sem, tick_sem, d_sem, p_sem, a_sem, wt_sem, g_sem, nd_sem, cv_sem, c2_sem, nn_sem, nz_sem,
 ):
     me = lax.axis_index("tm")
     z = lax.axis_index("nin")
@@ -79,6 +79,15 @@
     core = lax.rem(me, 2)
     half_own = lax.rem(chip, 2)
     mate = chip + 1 - 2 * half_own
+
+    def at(dy, c):
+        return lax.rem(chip + dy + TM // 2, TM // 2) * 2 + c
+
+    def ahead(peer):
+        return lax.rem(peer + TM - me, TM)
+
+    def behind(peer):
+        return lax.rem(me + TM - peer, TM)
 
     def x_peer(step):
         return lax.rem(xo + step, NOUT)
@@ -119,8 +128,6 @@
     ]
     for copy in blocks[0] + loads[:1]:
         copy.start()
-    for copy in loads[1:] + blocks[1]:
-        copy.start()
 
     barrier = pltpu.get_barrier_semaphore()
 
@@ -130,8 +137,8 @@
     def greet_z(step):
         pl.semaphore_signal(barrier, inc=1, device_id=(me, z_peer(step), xo), device_id_type=MESH)
 
-    each(1, TM, greet_tm)
-    each(1, NIN, greet_z)
+    far_first(TM, greet_tm)
+    far_first(NIN, greet_z)
 
     def greet_x(step):
         for c in range(2):
@@ -140,6 +147,8 @@
             )
 
     each(1, NOUT, greet_x)
+    for copy in loads[1:] + blocks[1]:
+        copy.start()
 
     for copy in blocks[0]:
         copy.wait()
@@ -215,6 +224,17 @@
         rows = pl.ds(pl.multiple_of(tm_peer(TM - step) * SLOT, SLOT), SLOT)
         return remote(d_send.at[0], d_all.at[:, rows, :], d_sem, step, tm_peer(step), z)
 
+    onward = [(-1, 0, 2), (1, 0, -2), (-1, 1, 2), (1, 1, -2), (-2, 0, 2), (2, 1, -2)]
+
+    def direction_onward(n):
+        dy, c, to = onward[n]
+        origin, target = at(dy, c), at(to, core)
+        rows = pl.ds(pl.multiple_of(origin * SLOT, SLOT), SLOT)
+        return pltpu.make_async_remote_copy(
+            src_ref=d_all.at[:, rows, :], dst_ref=d_all.at[:, rows, :], send_sem=on_sem.at[n],
+            recv_sem=d_sem.at[1, lax.rem(target + TM - origin, TM)], device_id=(target, z, xo), device_id_type=MESH,
+        )
+
     sends_halo = jnp.logical_and(part == GROUP - 1, team < TM // GROUP - 1)
     hands_halo = jnp.logical_and(core == 1, team > 0)
     spreads = [(step, other) for step in (2, 1, 3, 0) for other in range(2) if (step, other) != (0, 0)]
@@ -227,7 +247,10 @@
         halo_copy(1).start()
 
     core_copy().start()
-    far_first(TM, lambda step: direction_copy(step).start())
+    near = [(dy, c) for dy in (1, -1, 2, -2) for c in range(2)]
+    for dy, c in near:
+        direction_copy(ahead(at(dy, c))).start()
+    direction_copy(ahead(at(0, 1 - core))).start()
     each(1, GROUP, lambda step: tick_copy(step).start())
     d_all[:, d_rows, :] = d_send[part]
 
@@ -274,6 +297,10 @@
         for step, other in spreads:
             halo_spread(step, other).start()
 
+    for n, (dy, c, to) in enumerate(onward):
+        direction_arrival(behind(at(dy, c))).wait_recv()
+        direction_onward(n).start()
+
     def predictor(first, last):
         made = jnp.dot(x[first * HISTORY : last * HISTORY, :], wp[...], preferred_element_type=F32)
         made = made.reshape(last - first, NIN, 16, COLS)
@@ -312,7 +339,9 @@
     predictor(EARLY, 8)
     far_first(NIN, lambda step: predictor_copy(1, step).start())
 
-    each(1, TM, lambda step: direction_arrival(step).wait_recv())
+    direction_arrival(behind(at(0, 1 - core))).wait_recv()
+    for dy, c in ((-2, 1), (2, 0), (3, 0), (3, 1), (-3, 0), (-3, 1), (4, 0), (4, 1)):
+        direction_arrival(behind(at(dy, c))).wait_recv()
 
     def along_copy(half, step):
         blocks_of = slice(half * 4, half * 4 + 4)
@@ -463,7 +492,12 @@
             halo_spread(step, other).wait_send()
 
     each(1, GROUP, lambda step: tick_copy(step).wait_send())
-    for copy in (direction_copy, nd_copy, gram_copy, c2_copy, nn_copy):
+    for dy, c in near:
+        direction_copy(ahead(at(dy, c))).wait_send()
+    direction_copy(ahead(at(0, 1 - core))).wait_send()
+    for n in range(len(onward)):
+        direction_onward(n).wait_send()
+    for copy in (nd_copy, gram_copy, c2_copy, nn_copy):
         each(1, TM, lambda step: copy(step).wait_send())
     for copy in (cv_copy, nz_copy):
         each(1, NIN, lambda step: copy(step).wait_send())
@@ -519,6 +553,7 @@
         pltpu.VMEM((8, COLS), F32),
         pltpu.VMEM((NIN, 8, COLS), F32),
         pltpu.SemaphoreType.DMA((16,)),
+        pltpu.SemaphoreType.DMA((6,)),
         pair(9), pair(10), pair(GROUP),
         pair(TM), pair(2 * NIN), pair(2 * NIN), pair(2 * NIN), pair(TM),
         pair(TM), pair(NIN), pair(TM), pair(TM), pair(NIN),

time: 81.6 us -> 78.5 us (0.962)
  Pallas kernels: 78.8 us -> 75.7 us
    pallas_call x1, Pallas kernels: 78.8 us -> 75.7 us  [per_device(): pl.pallas_call(kernel, out_shape=[jax.ShapeDtypeStruct((rows, columns), F...]
where the time goes in v4:
time: 78.5 us; the launch traced here: 78.3 us
  Pallas kernels  75.7 us (96%)
  other arithmetic  1.92 us (2%)
    pallas_call x1, Pallas kernels, per_device(): pl.pallas_call(kernel, out_shape=[jax.ShapeDtypeStruct((rows, columns), F...  75.7 us
    add x1, other arithmetic, per_device(): new_residual + ratio * direction  1.92 us

profile of v4, /device:TPU:1, one launch (start us, length us, event | category | flops | bytes accessed | tf_op | source)
XLA Modules:
  0.0 78.3 jit_solution(10897517171515347064)
XLA Ops:
  0.6 0.0 copy-start.1
  0.6 0.0 copy-start
  0.7 0.0 copy-start.2
  0.7 75.7 %shard_map.103 = (f32[128,512]{1,0:T(8,128)}, f32[1,512]{1,0:T(1,128)}, f32[1,512]{1,0:T(1,128)}) custom-call(s32[2,128]{1,0:T(2,128)} %bitcast.5, s32[256,256]{1,0:T(8,128)} %spikes_hbm.1, bf16[2048,512]{1,0:T(8,128)(2,1)} %weights_hbm.1, f32[128,512]{1,0:T(8,128)} %direction_hbm.1, f32[128,512]{1,0:T(8,128)} %residual_hbm.1, ...), custom_call_target="tpu_custom_call" | custom-call | tf_op jit(solution)/shard_map/pallas_call | solution.py:561
  76.4 0.0 copy-done.1
  76.4 0.0 copy-done
  76.4 0.0 copy-done.2
  76.4 1.9 %multiply_add_fusion = (f32[128,512]{1,0:T(8,128)}, f32[128,512]{1,0:T(8,128)}, f32[128,512]{1,0:T(8,128)}) fusion(f32[128,512]{1,0:T(8,128)S(1)} %copy-done, f32[512]{0:T(512)} %bitcast.4, f32[128,512]{1,0:T(8,128)S(1)} %copy-done.1, f32[128,512]{1,0:T(8,128)} %get-tuple-element.7, f32[512]{0:T(512)} %bitcast.3, f32[128,512]{1,0:T(8,128)S(1)} %copy-done.2), kind=kLoop, calls=%fused_computation | loop fusion | flops 393216 | bytes 1839104 | tf_op jit(solution)/shard_map/add | solution.py:572
Async XLA Ops:
  0.6 75.7 %copy-start.1 = (f32[128,512]{1,0:T(8,128)S(1)}, f32[128,512]{1,0:T(8,128)}, u32[]{:S(2)}) copy-start(f32[128,512]{1,0:T(8,128)} %residual_hbm.1) | copy-start | bytes 786436
  0.6 75.7 %copy-start = (f32[128,512]{1,0:T(8,128)S(1)}, f32[128,512]{1,0:T(8,128)}, u32[]{:S(2)}) copy-start(f32[128,512]{1,0:T(8,128)} %direction_hbm.1) | copy-start | bytes 786436
  0.7 75.7 %copy-start.2 = (f32[128,512]{1,0:T(8,128)S(1)}, f32[128,512]{1,0:T(8,128)}, u32[]{:S(2)}) copy-start(f32[128,512]{1,0:T(8,128)} %param.13) | copy-start | bytes 786436

commit v5 on v4

--- a/solution.py
+++ b/solution.py
@@ -56,9 +56,9 @@
     exposure_ref, spikes_hbm, weights_hbm, direction_hbm, residual_hbm, lag_hbm, lag_t_hbm,
     product_out, step_out, ratio_out,
     spikes_in, lag, lag_t, d32, r32, w16, w32, wp, spk, spk_t, x, xt,
-    d_send, d_all, p_own, p_send, p_recv, a_own, a_send, a_recv, wt_all, g_send, g_recv, g_nat,
+    d_send, d_all, p_own, p_send, p_recv, a_own, a_send, a_recv, wt_all, g_send, g_recv, h_recv, g_nat,
     ticks, ticks_t, nd_send, nd_recv, cv_send, cv_recv, c2_send, c2_recv, nn_send, nn_recv, nz_send, nz_recv,
-    load_sem, on_sem, spk_sem, halo_sem, tick_sem, d_sem, p_sem, a_sem, wt_sem, g_sem, nd_sem, cv_sem, c2_sem, nn_sem, nz_sem,
+    load_sem, on_sem, spk_sem, halo_sem, tick_sem, d_sem, p_sem, a_sem, wt_sem, g_sem, h_sem, nd_sem, cv_sem, c2_sem, nn_sem, nz_sem,
 ):
     me = lax.axis_index("tm")
     z = lax.axis_index("nin")
@@ -316,6 +316,10 @@
     predictor(0, EARLY)
     far_first(NIN, lambda step: predictor_copy(0, step).start())
 
+    for dy in (3, 4, -3):
+        for c in range(2):
+            g_recv[at(dy, c)] = jnp.zeros((SLOT * BASES, COLS), BF16)
+
     for copy in blocks[1]:
         copy.wait()
     for k in range(GROUP):
@@ -397,31 +401,28 @@
     for half in range(2):
         each(1, NIN, lambda step: weighted_copy(half, z_peer(NIN - step), step).wait_recv())
 
-    def gram_copy(step):
-        return remote(g_send.at[tm_peer(step)], g_recv.at[me], g_sem, step, tm_peer(step), z)
-
     def gram_to(peer):
-        return remote(g_send.at[peer], g_recv.at[me], g_sem, lax.rem(peer + TM - me, TM), peer, z)
-
-    def gram_arrival(step):
-        return remote(g_send.at[0], g_recv.at[tm_peer(TM - step)], g_sem, step, tm_peer(step), z)
-
-    def gram(turn):
-        group = lax.rem(team + swing(turn, 2), GROUP)
-        rows = pl.ds(group * 4, 4)
+        return remote(g_send.at[peer], g_recv.at[me], g_sem, ahead(peer), peer, z)
+
+    def gram_from(peer):
+        return remote(g_send.at[0], g_recv.at[peer], g_sem, behind(peer), peer, z)
+
+    far = [(3, 0, 2), (3, 1, 2), (4, 0, 2), (-3, 0, -2), (-3, 1, -2), (-4, 1, -2)]
+
+    def gram_far(n):
+        dy, c, by = far[n]
+        return remote(g_send.at[at(dy, c)], h_recv.at[n], h_sem, n, at(by, core), z)
+
+    def gram(dy):
+        rows = pl.ds(pl.multiple_of(at(dy, 0), 2), 2)
         made = jnp.dot(
-            xt[rows].reshape(4 * SLOT * BASES, BINS), wt_all[...].reshape(BINS, COLS), preferred_element_type=F32
+            xt[rows].reshape(2 * SLOT * BASES, BINS), wt_all[...].reshape(BINS, COLS), preferred_element_type=F32
         )
-        g_send[rows] = made.astype(BF16).reshape(4, SLOT * BASES, COLS)
-
-        @pl.when(turn < 3)
-        def _():
-            each(0, GROUP, lambda k: gram_to(group * GROUP + k).start())
-
-    each(0, 4, gram)
-    each(1, GROUP, lambda step: gram_to(team_peer(step)).start())
-    g_recv[me] = g_send[me]
-
+        g_send[rows] = made.astype(BF16).reshape(2, SLOT * BASES, COLS)
+
+    each(0, 3, lambda turn: gram(3 + turn))
+    for n in (2, 5, 0, 3, 1, 4):
+        gram_far(n).start()
     each(1, NIN, lambda step: cv_copy(step).wait_recv())
     cv_sum = cv_send[...] + jnp.sum(cv_recv[1:NIN], axis=0)
     old_norm = cv_sum[0:4, :]
@@ -434,7 +435,19 @@
     def c2_arrival(step):
         return remote(c2_send, c2_recv.at[tm_peer(TM - step)], c2_sem, step, tm_peer(step), z)
 
-    each(1, TM, lambda step: c2_copy(step).start())
+    far_first(TM, lambda step: c2_copy(step).start())
+    each(0, 5, lambda turn: gram(turn - 2))
+    gram_to(at(2, 1)).start()
+    gram_to(at(-2, 0)).start()
+    gram_to(at(0, 1 - core)).start()
+    g_recv[me] = g_send[me]
+    for n in (2, 5, 0, 3, 1, 4):
+        dy, c, by = far[n]
+        target = at(dy - by, c)
+        gram_far(n).wait_recv()
+        g_send[target] = (g_send[target].astype(F32) + h_recv[n].astype(F32)).astype(BF16)
+        gram_to(target).start()
+
     each(1, TM, lambda step: c2_arrival(step).wait_recv())
     step_sizes = []
     for k in range(GROUP):
@@ -446,7 +459,9 @@
         step_sizes.append(step_size)
         step_out[:, k * COLS : (k + 1) * COLS] = step_size
 
-    each(1, TM, lambda step: gram_arrival(step).wait_recv())
+    gram_from(at(0, 1 - core)).wait_recv()
+    for dy, c in near:
+        gram_from(at(dy, c)).wait_recv()
     nn_send[4:8, :] = jnp.zeros((4, COLS), F32)
     for k in range(GROUP):
         total = g_recv[k].astype(F32)
@@ -497,7 +512,12 @@
     direction_copy(ahead(at(0, 1 - core))).wait_send()
     for n in range(len(onward)):
         direction_onward(n).wait_send()
-    for copy in (nd_copy, gram_copy, c2_copy, nn_copy):
+    for n in range(len(far)):
+        gram_far(n).wait_send()
+    for dy, c in near:
+        gram_to(at(dy, c)).wait_send()
+    gram_to(at(0, 1 - core)).wait_send()
+    for copy in (nd_copy, c2_copy, nn_copy):
         each(1, TM, lambda step: copy(step).wait_send())
     for copy in (cv_copy, nz_copy):
         each(1, NIN, lambda step: copy(step).wait_send())
@@ -539,6 +559,7 @@
         pltpu.VMEM((8, NIN, 16, COLS), BF16),
         pltpu.VMEM((TM, rows, COLS), BF16),
         pltpu.VMEM((TM, rows, COLS), BF16),
+        pltpu.VMEM((6, rows, COLS), BF16),
         pltpu.VMEM((GROUP, rows, COLS), F32),
         pltpu.VMEM((GROUP, 8, COLS), F32),
         pltpu.VMEM((COLS, COLS), F32),
@@ -555,7 +576,7 @@
         pltpu.SemaphoreType.DMA((16,)),
         pltpu.SemaphoreType.DMA((6,)),
         pair(9), pair(10), pair(GROUP),
-        pair(TM), pair(2 * NIN), pair(2 * NIN), pair(2 * NIN), pair(TM),
+        pair(TM), pair(2 * NIN), pair(2 * NIN), pair(2 * NIN), pair(TM), pair(6),
         pair(TM), pair(NIN), pair(TM), pair(TM), pair(NIN),
     ]
     product, step_size, ratio = pl.pallas_call(

time: 78.5 us -> 76.1 us (0.969)
  Pallas kernels: 75.7 us -> 73.3 us
    pallas_call x1, Pallas kernels: 75.7 us -> 73.3 us  [per_device(): pl.pallas_call(kernel, out_shape=[jax.ShapeDtypeStruct((rows, columns), F...]
where the time goes in v5:
time: 76.1 us; the launch traced here: 75.9 us
  Pallas kernels  73.3 us (96%)
  other arithmetic  1.92 us (3%)
    pallas_call x1, Pallas kernels, per_device(): pl.pallas_call(kernel, out_shape=[jax.ShapeDtypeStruct((rows, columns), F...  73.3 us
    add x1, other arithmetic, per_device(): new_residual + ratio * direction  1.92 us

profile of v5, /device:TPU:1, one launch (start us, length us, event | category | flops | bytes accessed | tf_op | source)
XLA Modules:
  0.0 75.9 jit_solution(16460087170246703757)
XLA Ops:
  0.6 0.0 copy-start.1
  0.6 0.0 copy-start
  0.7 0.0 copy-start.2
  0.7 73.3 %shard_map.103 = (f32[128,512]{1,0:T(8,128)}, f32[1,512]{1,0:T(1,128)}, f32[1,512]{1,0:T(1,128)}) custom-call(s32[2,128]{1,0:T(2,128)} %bitcast.5, s32[256,256]{1,0:T(8,128)} %spikes_hbm.1, bf16[2048,512]{1,0:T(8,128)(2,1)} %weights_hbm.1, f32[128,512]{1,0:T(8,128)} %direction_hbm.1, f32[128,512]{1,0:T(8,128)} %residual_hbm.1, ...), custom_call_target="tpu_custom_call" | custom-call | tf_op jit(solution)/shard_map/pallas_call | solution.py:582
  74.0 0.0 copy-done.1
  74.0 0.0 copy-done
  74.0 0.0 copy-done.2
  74.0 1.9 %multiply_add_fusion = (f32[128,512]{1,0:T(8,128)}, f32[128,512]{1,0:T(8,128)}, f32[128,512]{1,0:T(8,128)}) fusion(f32[128,512]{1,0:T(8,128)S(1)} %copy-done, f32[512]{0:T(512)} %bitcast.4, f32[128,512]{1,0:T(8,128)S(1)} %copy-done.1, f32[128,512]{1,0:T(8,128)} %get-tuple-element.7, f32[512]{0:T(512)} %bitcast.3, f32[128,512]{1,0:T(8,128)S(1)} %copy-done.2), kind=kLoop, calls=%fused_computation | loop fusion | flops 393216 | bytes 1839104 | tf_op jit(solution)/shard_map/add | solution.py:593
Async XLA Ops:
  0.6 73.4 %copy-start.1 = (f32[128,512]{1,0:T(8,128)S(1)}, f32[128,512]{1,0:T(8,128)}, u32[]{:S(2)}) copy-start(f32[128,512]{1,0:T(8,128)} %residual_hbm.1) | copy-start | bytes 786436
  0.6 73.4 %copy-start = (f32[128,512]{1,0:T(8,128)S(1)}, f32[128,512]{1,0:T(8,128)}, u32[]{:S(2)}) copy-start(f32[128,512]{1,0:T(8,128)} %direction_hbm.1) | copy-start | bytes 786436
  0.7 73.4 %copy-start.2 = (f32[128,512]{1,0:T(8,128)S(1)}, f32[128,512]{1,0:T(8,128)}, u32[]{:S(2)}) copy-start(f32[128,512]{1,0:T(8,128)} %param.13) | copy-start | bytes 786436

commit v6 on v5

--- a/solution.py
+++ b/solution.py
@@ -279,10 +279,6 @@
 
     loads[1].wait()
     loads[2].wait()
-    core_arrival().wait_recv()
-    each(0, 4, lambda k: turn_spikes(own_first + k))
-    each(0, EARLY, features)
-
     mate_arrival(0, 0).wait_recv()
     for step, other in spreads:
         spread_copy(step, other).start()
@@ -296,6 +292,10 @@
         halo_first().wait_recv()
         for step, other in spreads:
             halo_spread(step, other).start()
+
+    core_arrival().wait_recv()
+    each(0, 4, lambda k: turn_spikes(own_first + k))
+    each(0, EARLY, features)
 
     for n, (dy, c, to) in enumerate(onward):
         direction_arrival(behind(at(dy, c))).wait_recv()

time: 76.1 us -> 75.2 us (0.988)
  Pallas kernels: 73.3 us -> 72.4 us
    pallas_call x1, Pallas kernels: 73.3 us -> 72.4 us  [per_device(): pl.pallas_call(kernel, out_shape=[jax.ShapeDtypeStruct((rows, columns), F...]
where the time goes in v6:
time: 75.2 us; the launch traced here: 75 us
  Pallas kernels  72.4 us (96%)
  other arithmetic  1.92 us (3%)
    pallas_call x1, Pallas kernels, per_device(): pl.pallas_call(kernel, out_shape=[jax.ShapeDtypeStruct((rows, columns), F...  72.4 us
    add x1, other arithmetic, per_device(): new_residual + ratio * direction  1.92 us

profile of v6, /device:TPU:1, one launch (start us, length us, event | category | flops | bytes accessed | tf_op | source)
XLA Modules:
  0.0 75.0 jit_solution(1991564473127623036)
XLA Ops:
  0.6 0.0 copy-start.1
  0.6 0.0 copy-start
  0.7 0.0 copy-start.2
  0.7 72.4 %shard_map.103 = (f32[128,512]{1,0:T(8,128)}, f32[1,512]{1,0:T(1,128)}, f32[1,512]{1,0:T(1,128)}) custom-call(s32[2,128]{1,0:T(2,128)} %bitcast.5, s32[256,256]{1,0:T(8,128)} %spikes_hbm.1, bf16[2048,512]{1,0:T(8,128)(2,1)} %weights_hbm.1, f32[128,512]{1,0:T(8,128)} %direction_hbm.1, f32[128,512]{1,0:T(8,128)} %residual_hbm.1, ...), custom_call_target="tpu_custom_call" | custom-call | tf_op jit(solution)/shard_map/pallas_call | solution.py:582
  73.1 0.0 copy-done.1
  73.1 0.0 copy-done
  73.1 0.0 copy-done.2
  73.1 1.9 %multiply_add_fusion = (f32[128,512]{1,0:T(8,128)}, f32[128,512]{1,0:T(8,128)}, f32[128,512]{1,0:T(8,128)}) fusion(f32[128,512]{1,0:T(8,128)S(1)} %copy-done, f32[512]{0:T(512)} %bitcast.4, f32[128,512]{1,0:T(8,128)S(1)} %copy-done.1, f32[128,512]{1,0:T(8,128)} %get-tuple-element.7, f32[512]{0:T(512)} %bitcast.3, f32[128,512]{1,0:T(8,128)S(1)} %copy-done.2), kind=kLoop, calls=%fused_computation | loop fusion | flops 393216 | bytes 1839104 | tf_op jit(solution)/shard_map/add | solution.py:593
Async XLA Ops:
  0.6 72.5 %copy-start.1 = (f32[128,512]{1,0:T(8,128)S(1)}, f32[128,512]{1,0:T(8,128)}, u32[]{:S(2)}) copy-start(f32[128,512]{1,0:T(8,128)} %residual_hbm.1) | copy-start | bytes 786436
  0.6 72.5 %copy-start = (f32[128,512]{1,0:T(8,128)S(1)}, f32[128,512]{1,0:T(8,128)}, u32[]{:S(2)}) copy-start(f32[128,512]{1,0:T(8,128)} %direction_hbm.1) | copy-start | bytes 786436
  0.7 72.5 %copy-start.2 = (f32[128,512]{1,0:T(8,128)S(1)}, f32[128,512]{1,0:T(8,128)}, u32[]{:S(2)}) copy-start(f32[128,512]{1,0:T(8,128)} %param.13) | copy-start | bytes 786436
